TPU v7x, 32 devices: a whole 2x2x4 slice. The times are simulated.
32 devices in a mesh: groups: 2 (over x), lib: 16 (over z, y, core).
Axes of the slice: x: 2, y: 2, z: 4, core: 2. Of those that a mesh axis runs over, the one named last changes fastest.
Arguments:
- spectra: bfloat16 [512, 4096], P(('groups', 'lib')), parts along dimension 0, may hold values from -6 to 6
- library: bfloat16 [8192, 4096], P('lib'), may hold values from -6 to 6
- cand_block: int32 [512, 8], P(('groups', 'lib')), parts along dimension 0, may hold values from 0 to 15, all different within a row; in each aligned block of 16 rows (0 to 15, 16 to 31, ...) at most 12 rows name the same one
- cand_local: int32 [512, 8, 8], P(('groups', 'lib')), parts along dimension 0, may hold values from 0 to 511
Outputs:
- profiles: float32 [512, 64, 1024], P(('groups', 'lib')), parts along dimension 0
There are 2 independent parts, one for each index of `groups`. A program takes and returns all parts, laid end to end along the dimension named above; an argument that names none is the same for every part. Nothing has to cross between parts.
Inputs may be any that keep to these rules, and one draw needn't show every extreme that they name: `cand_block`: each query names 8 different blocks; among the 16 queries of one device no block is named by more than 12 of them, and 12 is reached.
All inputs are finite; a program needn't handle non-finite values.
Results may differ from a plain program's by a relative error of at most 0.0029.
Values may be sent and summed in bfloat16 or wider, within the bound.
No kernel may reach another device: no remote copies, remote signals or barrier semaphores. Data moves between devices by JAX's collectives and lax.ppermute only.
A program may use at most 128 MiB of HBM per device.

v0:
```python
import math

import jax
import jax.numpy as jnp
from jax import lax
from jax.sharding import PartitionSpec as P

SHIFTS = 1024
BG = 32


EPSILON = 1e-06


def prepare(spectra):
    values = spectra.astype(jnp.float32)
    window_sum = lax.reduce_window(
        values, jnp.float32(0.0), lax.add, (1, 2 * BG + 1), (1, 1), ((0, 0), (BG, BG))
    )
    centered = values - window_sum / (2 * BG + 1)
    factor = lax.rsqrt(jnp.mean(centered * centered, axis=1, keepdims=True) + EPSILON)
    return (centered * factor).astype(jnp.bfloat16)


def hankel_of(prepared):
    num_query, num_bins = prepared.shape
    width_ext = num_bins + 128
    extended = jnp.concatenate([prepared, jnp.zeros((num_query, 129), prepared.dtype)], axis=1)
    tiled = jnp.tile(extended, (1, 128))[:, : 128 * width_ext]
    return tiled.reshape(num_query, 128, width_ext)


def rank_among(blocks):
    length = blocks.shape[0]
    same_block = blocks[:, None] == blocks[None, :]
    earlier = jnp.arange(length)[:, None] > jnp.arange(length)[None, :]
    return jnp.sum(same_block & earlier, axis=1)


def correlate(operands):
    prepared, cand_rows = operands
    num_query, num_cand = (cand_rows.shape[0], cand_rows.shape[1])
    hankel = hankel_of(prepared)
    width_ext = hankel.shape[2]
    padded = jnp.pad(cand_rows, ((0, 0), (0, 0), (SHIFTS // 2, SHIFTS // 2)))
    stacked = jnp.stack(
        [padded[:, :, 128 * offset : 128 * offset + width_ext] for offset in range(SHIFTS // 128)],
        axis=2,
    )
    stacked = stacked.reshape(num_query, -1, width_ext)
    values = jnp.einsum("qmw,qrw->qmr", stacked, hankel, preferred_element_type=jnp.float32)
    return values.reshape(num_query, num_cand, SHIFTS)


def profiles_of(prepared, cand_rows):
    num_items, num_cand, num_bins = cand_rows.shape
    scales = lax.rsqrt(jnp.mean(jnp.square(cand_rows.astype(jnp.float32)), axis=2) + EPSILON)
    group_size = math.gcd(num_items, 4)
    folded = lax.map(
        correlate,
        (
            prepared.reshape(-1, group_size, num_bins),
            cand_rows.reshape(-1, group_size, num_cand, num_bins),
        ),
    )
    return folded.reshape(num_items, num_cand, SHIFTS) * scales[:, :, None]


def local(spectra, library, cand_block, cand_local):
    devices = lax.axis_size("lib")
    num_query, num_bins = spectra.shape
    touches = cand_block.shape[1]
    per_touch = cand_local.shape[2]
    depth = min(num_query, max(3, 3 * num_query * touches // (2 * devices)))
    flat_block = cand_block.reshape(-1)
    slot_of = flat_block * depth + rank_among(flat_block)
    requests = (
        jnp.zeros((devices * depth, per_touch), jnp.int32)
        .at[slot_of]
        .set(cand_local.reshape(-1, per_touch))
    )
    incoming = lax.all_to_all(
        requests.reshape(devices, depth, per_touch), "lib", split_axis=0, concat_axis=0, tiled=True
    )
    picked = library[incoming.reshape(-1)].reshape(devices, depth, per_touch, num_bins)
    prepared = prepare(spectra)
    returned = lax.all_to_all(picked, "lib", split_axis=0, concat_axis=0, tiled=True)
    cand_rows = returned.reshape(devices * depth, per_touch, num_bins)[slot_of]
    cand_rows = cand_rows.reshape(num_query, touches * per_touch, num_bins)
    return profiles_of(prepared, cand_rows)


def solution(mesh):
    placed = (
        P(("groups", "lib"), None),
        P("lib", None),
        P(("groups", "lib"), None),
        P(("groups", "lib"), None, None),
    )
    return jax.shard_map(
        local,
        mesh=mesh,
        in_specs=placed,
        out_specs=P(("groups", "lib"), None, None),
        check_vma=False,
    )
```

profile of v0, /device:TPU:13, one launch (start us, length us, event | category | flops | bytes accessed | tf_op | source)
XLA Modules:
  0.0 549.6 jit_solution(4667895603498914657)
XLA Ops:
  3.9 10.6 %all_to_all.10 = s32[16,12,8]{1,2,0:T(8,128)S(1)} all-to-all(s32[16,12,8]{1,2,0:T(8,128)S(1)} %copy.40), channel_id=1, replica_groups=mesh['groups'=2,'lib'=16] {'lib'}, dimensions={0} | all-to-all | bytes 12288 | tf_op jit(solution)/shard_map/all_to_all | solution.py:82
  14.8 24.8 %gather_fusion = bf16[1536,4096]{1,0:T(8,128)(2,1)} fusion(bf16[512,4096]{1,0:T(8,128)(2,1)} %param.7, s32[2048]{0:T(1024)S(1)} %pad_clamp_fusion), kind=kCustom, calls=%fused_computation | custom fusion | bytes 25171968 | tf_op jit(solution)/shard_map/gather | solution.py:85
  39.6 7.8 %all-to-all-start.1 = ((bf16[16,12,8,4096]{3,2,1,0:T(8,128)(2,1)}), bf16[16,12,8,4096]{3,2,1,0:T(8,128)(2,1)}, u32[]{:S(2)}, u32[]{:S(2)}) async-start(bf16[16,12,8,4096]{3,2,1,0:T(8,128)(2,1)} %bitcast.87), calls=%async_computation.1 | async-start | bytes 25165824 | tf_op jit(solution)/shard_map/all_to_all | solution.py:87
  47.4 36.4 %reduce_window.7 = f32[16,4096]{1,0:T(8,128)S(1)} reduce-window(bf16[16,4096]{1,0:T(8,128)(2,1)S(1)} %copy-done.1, f32[]{:T(128)} %constant.46.clone.1), window={size=1x65 pad=0_0x32_32}, to_apply=%region_0.0 | reduce-window | flops 4194304 | bytes 393220 | tf_op jit(solution)/shard_map/reduce_window | solution.py:17
  84.2 235.2 %all-to-all-done.1 = bf16[16,12,8,4096]{3,2,1,0:T(8,128)(2,1)} async-done(((bf16[16,12,8,4096]{3,2,1,0:T(8,128)(2,1)}), bf16[16,12,8,4096]{3,2,1,0:T(8,128)(2,1)}, u32[]{:S(2)}, u32[]{:S(2)}) %all-to-all-start.1) | async-done | bytes 12582944 | tf_op jit(solution)/shard_map/all_to_all | solution.py:87
  319.4 11.2 %gather_fusion.1 = bf16[128,8,4096]{2,1,0:T(8,128)(2,1)} fusion(bf16[192,8,4096]{2,1,0:T(8,128)(2,1)} %bitcast.15, s32[1024]{0:T(1024)S(1)} %pad_clamp_fusion.1), kind=kCustom, calls=%fused_computation.1 | custom fusion | bytes 16777728 | tf_op jit(solution)/shard_map/gather | solution.py:88
  330.6 5.7 %multiply_reduce_fusion = f32[128,8]{1,0:T(8,128)} fusion(bf16[128,8,4096]{2,1,0:T(8,128)(2,1)} %gather_fusion.1), kind=kLoop, calls=%fused_computation.35 | loop fusion | flops 12581888 | bytes 8392704 | tf_op jit(solution)/shard_map/reduce_sum | solution.py:57
  336.3 208.5 %while.12 = (s32[]{:T(128)}, f32[4,4,64,1024]{3,2,1,0:T(8,128)}, bf16[4,4,64,4096]{3,2,1,0:T(8,128)(2,1)}, bf16[4,4,4096]{2,1,0:T(4,128)(2,1)S(1)}, s32[]{:T(128)}, /*index=5*/bf16[]{:T(256)}) while((s32[]{:T(128)}, f32[4,4,64,1024]{3,2,1,0:T(8,128)}, bf16[4,4,64,4096]{3,2,1,0:T(8,128)(2,1)}, bf16[4,4,4096]{2,1,0:T(4,128)(2,1)S(1)}, ...), condition=%wide.region_5.6_spmd, body=%wide.region_4.0_spmd.sunk | while | flops 2214592512 | bytes 169123488 | solution.py:59
  340.9 5.9 %copy-done = bf16[4,64,8,4224]{3,1,0,2:T(8,128)(2,1)} copy-done((bf16[4,64,8,4224]{3,1,0,2:T(8,128)(2,1)}, bf16[4,64,8,4224]{3,1,0,2:T(8,128)(2,1)S(1)}, u32[]{:S(2)}) %copy-start) | copy-done | bytes 17301528 | tf_op jit(solution)/shard_map/while
  346.8 2.4 tile.14
  349.2 10.0 %reshape.158 = bf16[2163200]{0:T(1024)(128)(2,1)} reshape(bf16[4,128,4225]{2,1,0:T(8,128)(2,1)} %tile.14) | data formatting | bytes 8652800 | tf_op jit(solution)/shard_map/while
  359.2 8.8 %tile.15 = bf16[4,540800]{1,0:T(4,128)(2,1)} reshape(bf16[2163200]{0:T(1024)(128)(2,1)} %reshape.158) | data formatting | bytes 8652800 | tf_op jit(solution)/shard_map/while/body/eval_jaxpr/tile | solution.py:29
  368.0 2.2 slice-done
  370.2 17.3 %fusion.48 = f32[4,512,128]{2,1,0:T(8,128)S(1)} fusion(bf16[4,64,8,4224]{3,1,0,2:T(8,128)(2,1)} %copy-done, bf16[1,4,128,4224]{3,1,2,0:T(4,128)(2,1)S(1)} %bitcast.85), kind=kOutput, calls=%fused_computation.3.clone.1 | convolution fusion | flops 2214592512 | bytes 22675456 | tf_op jit(solution)/shard_map/while/body/eval_jaxpr/qmw,qrw->qmr/dot_general | solution.py:51
  392.9 5.9 %copy-done = bf16[4,64,8,4224]{3,1,0,2:T(8,128)(2,1)} copy-done((bf16[4,64,8,4224]{3,1,0,2:T(8,128)(2,1)}, bf16[4,64,8,4224]{3,1,0,2:T(8,128)(2,1)S(1)}, u32[]{:S(2)}) %copy-start) | copy-done | bytes 17301528 | tf_op jit(solution)/shard_map/while
  398.8 2.4 tile.14
  401.3 10.0 %reshape.158 = bf16[2163200]{0:T(1024)(128)(2,1)} reshape(bf16[4,128,4225]{2,1,0:T(8,128)(2,1)} %tile.14) | data formatting | bytes 8652800 | tf_op jit(solution)/shard_map/while
  411.2 8.8 %tile.15 = bf16[4,540800]{1,0:T(4,128)(2,1)} reshape(bf16[2163200]{0:T(1024)(128)(2,1)} %reshape.158) | data formatting | bytes 8652800 | tf_op jit(solution)/shard_map/while/body/eval_jaxpr/tile | solution.py:29
  420.0 2.2 slice-done
  422.3 17.3 %fusion.48 = f32[4,512,128]{2,1,0:T(8,128)S(1)} fusion(bf16[4,64,8,4224]{3,1,0,2:T(8,128)(2,1)} %copy-done, bf16[1,4,128,4224]{3,1,2,0:T(4,128)(2,1)S(1)} %bitcast.85), kind=kOutput, calls=%fused_computation.3.clone.1 | convolution fusion | flops 2214592512 | bytes 22675456 | tf_op jit(solution)/shard_map/while/body/eval_jaxpr/qmw,qrw->qmr/dot_general | solution.py:51
  444.9 5.9 %copy-done = bf16[4,64,8,4224]{3,1,0,2:T(8,128)(2,1)} copy-done((bf16[4,64,8,4224]{3,1,0,2:T(8,128)(2,1)}, bf16[4,64,8,4224]{3,1,0,2:T(8,128)(2,1)S(1)}, u32[]{:S(2)}) %copy-start) | copy-done | bytes 17301528 | tf_op jit(solution)/shard_map/while
  450.9 2.4 tile.14
  453.3 10.0 %reshape.158 = bf16[2163200]{0:T(1024)(128)(2,1)} reshape(bf16[4,128,4225]{2,1,0:T(8,128)(2,1)} %tile.14) | data formatting | bytes 8652800 | tf_op jit(solution)/shard_map/while
  463.3 8.8 %tile.15 = bf16[4,540800]{1,0:T(4,128)(2,1)} reshape(bf16[2163200]{0:T(1024)(128)(2,1)} %reshape.158) | data formatting | bytes 8652800 | tf_op jit(solution)/shard_map/while/body/eval_jaxpr/tile | solution.py:29
  472.1 2.2 slice-done
  474.3 17.3 %fusion.48 = f32[4,512,128]{2,1,0:T(8,128)S(1)} fusion(bf16[4,64,8,4224]{3,1,0,2:T(8,128)(2,1)} %copy-done, bf16[1,4,128,4224]{3,1,2,0:T(4,128)(2,1)S(1)} %bitcast.85), kind=kOutput, calls=%fused_computation.3.clone.1 | convolution fusion | flops 2214592512 | bytes 22675456 | tf_op jit(solution)/shard_map/while/body/eval_jaxpr/qmw,qrw->qmr/dot_general | solution.py:51
  497.0 5.9 %copy-done = bf16[4,64,8,4224]{3,1,0,2:T(8,128)(2,1)} copy-done((bf16[4,64,8,4224]{3,1,0,2:T(8,128)(2,1)}, bf16[4,64,8,4224]{3,1,0,2:T(8,128)(2,1)S(1)}, u32[]{:S(2)}) %copy-start) | copy-done | bytes 17301528 | tf_op jit(solution)/shard_map/while
  502.9 2.4 tile.14
  505.3 10.0 %reshape.158 = bf16[2163200]{0:T(1024)(128)(2,1)} reshape(bf16[4,128,4225]{2,1,0:T(8,128)(2,1)} %tile.14) | data formatting | bytes 8652800 | tf_op jit(solution)/shard_map/while
  515.3 8.8 %tile.15 = bf16[4,540800]{1,0:T(4,128)(2,1)} reshape(bf16[2163200]{0:T(1024)(128)(2,1)} %reshape.158) | data formatting | bytes 8652800 | tf_op jit(solution)/shard_map/while/body/eval_jaxpr/tile | solution.py:29
  526.3 17.3 %fusion.48 = f32[4,512,128]{2,1,0:T(8,128)S(1)} fusion(bf16[4,64,8,4224]{3,1,0,2:T(8,128)(2,1)} %copy-done, bf16[1,4,128,4224]{3,1,2,0:T(4,128)(2,1)S(1)} %bitcast.85), kind=kOutput, calls=%fused_computation.3.clone.1 | convolution fusion | flops 2214592512 | bytes 22675456 | tf_op jit(solution)/shard_map/while/body/eval_jaxpr/qmw,qrw->qmr/dot_general | solution.py:51
  545.0 4.5 bitcast_multiply_fusion
  (89 shorter events, 28.1 us)
Async XLA Ops:
  39.6 7.8 %copy-start.1 = (bf16[16,4096]{1,0:T(8,128)(2,1)S(1)}, bf16[16,4096]{1,0:T(8,128)(2,1)}, u32[]{:S(2)}) copy-start(bf16[16,4096]{1,0:T(8,128)(2,1)} %param.6) | copy-start | bytes 393220
  39.6 279.8 %all-to-all-start.1 = ((bf16[16,12,8,4096]{3,2,1,0:T(8,128)(2,1)}), bf16[16,12,8,4096]{3,2,1,0:T(8,128)(2,1)}, u32[]{:S(2)}, u32[]{:S(2)}) async-start(bf16[16,12,8,4096]{3,2,1,0:T(8,128)(2,1)} %bitcast.87), calls=%async_computation.1 | async-start | bytes 25165824 | tf_op jit(solution)/shard_map/all_to_all | solution.py:87
  336.3 208.5 %copy-start.2 = (f32[128,8]{1,0:T(8,128)S(1)}, f32[128,8]{1,0:T(8,128)}, u32[]{:S(2)}) copy-start(f32[128,8]{1,0:T(8,128)} %multiply_reduce_fusion) | copy-start | bytes 12292
  340.9 5.9 %copy-start = (bf16[4,64,8,4224]{3,1,0,2:T(8,128)(2,1)}, bf16[4,64,8,4224]{3,1,0,2:T(8,128)(2,1)S(1)}, u32[]{:S(2)}) copy-start(bf16[4,64,8,4224]{3,1,0,2:T(8,128)(2,1)S(1)} %fusion.47) | copy-start | bytes 51904516 | tf_op jit(solution)/shard_map/while
  368.0 2.2 slice-start
  392.9 5.9 %copy-start = (bf16[4,64,8,4224]{3,1,0,2:T(8,128)(2,1)}, bf16[4,64,8,4224]{3,1,0,2:T(8,128)(2,1)S(1)}, u32[]{:S(2)}) copy-start(bf16[4,64,8,4224]{3,1,0,2:T(8,128)(2,1)S(1)} %fusion.47) | copy-start | bytes 51904516 | tf_op jit(solution)/shard_map/while
  420.0 2.2 slice-start
  444.9 5.9 %copy-start = (bf16[4,64,8,4224]{3,1,0,2:T(8,128)(2,1)}, bf16[4,64,8,4224]{3,1,0,2:T(8,128)(2,1)S(1)}, u32[]{:S(2)}) copy-start(bf16[4,64,8,4224]{3,1,0,2:T(8,128)(2,1)S(1)} %fusion.47) | copy-start | bytes 51904516 | tf_op jit(solution)/shard_map/while
  472.1 2.2 slice-start
  497.0 5.9 %copy-start = (bf16[4,64,8,4224]{3,1,0,2:T(8,128)(2,1)}, bf16[4,64,8,4224]{3,1,0,2:T(8,128)(2,1)S(1)}, u32[]{:S(2)}) copy-start(bf16[4,64,8,4224]{3,1,0,2:T(8,128)(2,1)S(1)} %fusion.47) | copy-start | bytes 51904516 | tf_op jit(solution)/shard_map/while
  524.1 2.2 slice-start
where the time goes:
time: 555 us; the launch traced here: 550 us
  waiting for transfers between devices  235 us (42%)
  local copies, waits for them, and re-layouts  178 us (32%)
  matrix products  69.2 us (12%)
  other arithmetic  47.9 us (9%)
  blocking collectives  10.6 us (2%)
  starting transfers between devices  7.81 us (1%)
    all_to_all x1, waiting for transfers between devices, local(): lax.all_to_all(picked, 'lib', split_axis=0, concat_axis=0, tiled=True)  235 us
    while x40, local copies, waits for them, and re-layouts  71.7 us
    dot_general x4, matrix products, correlate(): jnp.einsum('qmw,qrw->qmr', stacked, hankel, preferred_element_type=jnp.fl...  69.2 us
    another operation x8, local copies, waits for them, and re-layouts, hankel_of(): tiled = jnp.tile(extended, (1, 128))[:, :128 * width_ext]  44.9 us
    another operation x1, other arithmetic, prepare(): lax.reduce_window(values, jnp.float32(0.0), lax.add, (1, 2 * BG + 1), (1,...  36.4 us
    gather x1, local copies, waits for them, and re-layouts, local(): library[incoming.reshape(-1)].reshape(devices, depth, per_touch, num_bins)  24.8 us
    gather x1, local copies, waits for them, and re-layouts, local(): cand_rows = returned.reshape(devices * depth, per_touch, num_bins)[slot_of]  11.2 us
  transfers between devices with their start and end apart: 1, of which 1 were waited for; matrix products, arithmetic and copies ran while one was open for 7% of the time, Pallas kernels for 0%

commit v1 on v0

v1 whole, which is shorter than its diff:
```python
import functools

import jax
import jax.numpy as jnp
from jax import lax
from jax.experimental import pallas as pl
from jax.experimental.pallas import tpu as pltpu
from jax.sharding import PartitionSpec as P

SHIFTS = 1024
BG = 32
EPSILON = 1e-06
LANES = 128
VMEM_LIMIT = 48 * 1024 * 1024
PARTS = 3


def depth_of(num_query, touches, devices):
    return min(num_query, max(3, 3 * num_query * touches // (2 * devices)))


def prepare_kernel(spectra_ref, out_ref, rows_ref):
    num_query, num_bins = spectra_ref.shape
    blocks = num_bins // LANES
    values = spectra_ref[...].astype(jnp.float32)
    zeros = jnp.zeros((num_query, LANES), jnp.float32)
    wide = jnp.concatenate([values, zeros], axis=1)
    total, length = wide, 1
    while length < 2 * BG:
        total = total + pltpu.roll(total, length, 1)
        length *= 2
    total = total + pltpu.roll(wide, length, 1)
    total = pltpu.roll(total, total.shape[1] - BG, 1)[:, :num_bins]
    centered = values - total / (2 * BG + 1)
    factor = lax.rsqrt(jnp.mean(centered * centered, axis=1, keepdims=True) + EPSILON)
    prepared = (centered * factor).astype(jnp.bfloat16)
    row = lax.broadcasted_iota(jnp.int32, (LANES, LANES), 0)
    col = lax.broadcasted_iota(jnp.int32, (LANES, LANES), 1)
    flip = jnp.where(row + col == LANES - 1, 1.0, 0.0).astype(jnp.bfloat16)
    for block in range(blocks):
        piece = prepared[:, block * LANES : (block + 1) * LANES]
        turned = jnp.dot(piece, flip, preferred_element_type=jnp.float32)
        rows_ref[pl.ds(blocks - 1 - block, num_query, stride=blocks), :] = turned
    out_ref[...] = rows_ref[...].reshape(out_ref.shape).astype(jnp.bfloat16)


def prepare(spectra):
    num_query, num_bins = spectra.shape
    blocks = num_bins // LANES
    return pl.pallas_call(
        prepare_kernel,
        out_shape=jax.ShapeDtypeStruct((num_query, blocks, LANES), jnp.bfloat16),
        scratch_shapes=[pltpu.VMEM((num_query * blocks, LANES), jnp.float32)],
        compiler_params=pltpu.CompilerParams(vmem_limit_bytes=VMEM_LIMIT),
        name="prepare",
    )(spectra)


def route_kernel(num_query, touches, depth, me_ref, named_ref, own_ref, slots_ref, returns_ref):
    me = me_ref[0]
    slots = slots_ref.shape[0] - 1
    devices = slots // depth

    @pl.loop(0, slots + 1)
    def _(i):
        slots_ref[i] = -1
        returns_ref[i] = -1

    @pl.loop(0, devices)
    def _(device):
        first = device * num_query

        def query(q, place):
            for t in range(touches):
                touch = (first + q) * touches + t
                hit = named_ref[touch] == me
                slots_ref[place] = jnp.where(hit, touch, -1)
                place = place + hit.astype(jnp.int32)
            return place

        lax.fori_loop(0, num_query, query, device * depth)

    @pl.loop(0, num_query)
    def _(q):
        for t in range(touches):
            touch = q * touches + t
            base = own_ref[touch] * depth
            taken = jnp.int32(0)
            for s in range(depth):
                taken = taken + (returns_ref[base + s] >= 0).astype(jnp.int32)
            returns_ref[base + taken] = touch


def route(me, named, own, num_query, touches, depth):
    devices = named.shape[0] // (num_query * touches)
    smem = pl.BlockSpec(memory_space=pltpu.SMEM)
    table = jax.ShapeDtypeStruct((devices * depth + 1,), jnp.int32)
    return pl.pallas_call(
        functools.partial(route_kernel, num_query, touches, depth),
        out_shape=(table, table),
        in_specs=[smem] * 3,
        out_specs=(smem, smem),
        name="route",
    )(me, named, own)


def profile_kernel(
    part, depth, touches, slots_ref, local_ref, query_ref, library_ref, out_ref,
    cand_ref, left_ref, right_ref,
):
    per_touch = 8
    blocks = query_ref.shape[1]
    offsets = SHIFTS // LANES
    edge = offsets // 2
    part_depth = depth // PARTS
    part_slots = out_ref.shape[0] // per_touch
    tiles = (blocks + 2) // 2
    row = lax.broadcasted_iota(jnp.int32, (8, LANES), 0)
    lane = lax.broadcasted_iota(jnp.int32, (8, LANES), 1)
    lane16 = lax.broadcasted_iota(jnp.int32, (16, LANES), 1)

    cand_ref[...] = jnp.zeros(cand_ref.shape, cand_ref.dtype)
    right_ref[...] = jnp.zeros(right_ref.shape, right_ref.dtype)

    def one(slot, half):
        place = slot // part_depth * depth + part * part_depth + slot % part_depth
        touch = jnp.maximum(slots_ref[place], 0)
        square = jnp.zeros((per_touch, LANES), jnp.float32)
        for k in range(per_touch):
            wanted = local_ref[touch * per_touch + k]
            cand_ref[half, pl.ds(edge * per_touch + k, blocks, stride=per_touch), :] = (
                library_ref[wanted].astype(jnp.float32)
            )
        for b in range(blocks):
            piece = cand_ref[half, pl.ds((edge + b) * per_touch, per_touch), :]
            square = square + piece * piece
        mean = jnp.sum(square, axis=1, keepdims=True) / (blocks * LANES)
        scale = lax.rsqrt(mean + EPSILON)
        for g in range((blocks + offsets) // 2):
            left_ref[half, pl.ds(16 * g, 16), 0:LANES] = cand_ref[
                half, pl.ds(16 * g, 16), :
            ].astype(jnp.bfloat16)
            left_ref[half, pl.ds(16 * g, 16), LANES : 2 * LANES] = cand_ref[
                half, pl.ds(16 * g + 8, 16), :
            ].astype(jnp.bfloat16)

        spectrum = query_ref[touch // touches].astype(jnp.float32)
        zero = jnp.zeros((8, LANES), jnp.float32)
        before = (zero, zero)
        before_shifted = jnp.zeros((16, LANES), jnp.bfloat16)
        for b in range(blocks + 1):
            if b < blocks:
                wide = jnp.broadcast_to(spectrum[b : b + 1, :], (8, LANES))
                now = tuple(
                    pltpu.roll(wide, 1 + 8 * h, 1, stride=1, stride_axis=0) for h in range(2)
                )
            else:
                now = (zero, zero)
            shifted = jnp.concatenate(
                [jnp.where(lane > row + 8 * h, now[h], before[h]) for h in range(2)], axis=0
            ).astype(jnp.bfloat16)
            for a in range(8):
                if a == 0:
                    tile = shifted
                else:
                    tile = pltpu.roll(
                        jnp.where(lane16 < LANES - 16 * a, shifted, before_shifted), 16 * a, 1
                    )
                right_ref[half, pl.ds((blocks - b) * LANES + 16 * a, 16), :] = tile
            before, before_shifted = now, shifted

        left = jnp.concatenate(
            [left_ref[half, pl.ds(16 * u, 8 * offsets), :] for u in range(tiles)], axis=1
        )
        product = jnp.dot(left, right_ref[half], preferred_element_type=jnp.float32)
        return [product[8 * o : 8 * o + 8, :] * scale for o in range(offsets)]

    @pl.loop(0, part_slots // 2)
    def _(pair):
        first = one(2 * pair, 0)
        second = one(2 * pair + 1, 1)
        for o in range(offsets):
            out_ref[pl.ds(pl.multiple_of(16 * pair, 16), 16), o * LANES : (o + 1) * LANES] = (
                jnp.concatenate([first[o], second[o]], axis=0).astype(jnp.bfloat16)
            )


def profile(part, depth, touches, devices, slots, local, queries, library):
    blocks = queries.shape[1]
    offsets = SHIFTS // LANES
    part_slots = devices * depth // PARTS
    rows = (blocks + offsets + 2) * 8
    smem = pl.BlockSpec(memory_space=pltpu.SMEM)
    vmem = pl.BlockSpec(memory_space=pltpu.VMEM)
    flops = part_slots * 2 * 8 * offsets * (blocks + 2) * LANES * LANES
    return pl.pallas_call(
        functools.partial(profile_kernel, part, depth, touches),
        out_shape=jax.ShapeDtypeStruct((part_slots * 8, SHIFTS), jnp.bfloat16),
        in_specs=[smem, smem, vmem, vmem],
        out_specs=vmem,
        scratch_shapes=[
            pltpu.VMEM((2, rows, LANES), jnp.float32),
            pltpu.VMEM((2, (blocks + offsets) * 8, 2 * LANES), jnp.bfloat16),
            pltpu.VMEM((2, (blocks + 2) * LANES, LANES), jnp.bfloat16),
        ],
        compiler_params=pltpu.CompilerParams(vmem_limit_bytes=VMEM_LIMIT),
        cost_estimate=pl.CostEstimate(
            flops=8 * flops, bytes_accessed=8 * 1024 * 1024, transcendentals=0
        ),
        name=f"profile_{part}",
    )(slots, local, queries, library)


def unpack_kernel(part, depth, returns_ref, got_ref, *rest):
    out_ref, stage_ref, sem_ref = rest[-3:]
    part_depth = depth // PARTS
    slots = got_ref.shape[0]

    def copy(slot, touch):
        return pltpu.make_async_copy(stage_ref.at[slot], out_ref.at[touch], sem_ref.at[slot])

    def touch_of(slot):
        return returns_ref[slot // part_depth * depth + part * part_depth + slot % part_depth]

    @pl.loop(0, slots)
    def _(slot):
        touch = touch_of(slot)

        @pl.when(touch >= 0)
        def _():
            stage_ref[slot] = got_ref[slot].astype(jnp.float32)
            copy(slot, touch).start()

    @pl.loop(0, slots)
    def _(slot):
        touch = touch_of(slot)

        @pl.when(touch >= 0)
        def _():
            copy(slot, touch).wait()


def unpack(part, depth, touched, returns, got, out):
    slots, per_touch, shifts = got.shape
    smem = pl.BlockSpec(memory_space=pltpu.SMEM)
    vmem = pl.BlockSpec(memory_space=pltpu.VMEM)
    hbm = pl.BlockSpec(memory_space=pl.ANY)
    more = () if out is None else (out,)
    return pl.pallas_call(
        functools.partial(unpack_kernel, part, depth),
        out_shape=jax.ShapeDtypeStruct((touched, per_touch, shifts), jnp.float32),
        in_specs=[smem, vmem] + [hbm] * len(more),
        out_specs=hbm,
        scratch_shapes=[
            pltpu.VMEM((slots, per_touch, shifts), jnp.float32),
            pltpu.SemaphoreType.DMA((slots,)),
        ],
        input_output_aliases={2: 0} if more else {},
        compiler_params=pltpu.CompilerParams(vmem_limit_bytes=VMEM_LIMIT),
        cost_estimate=pl.CostEstimate(
            flops=0, bytes_accessed=got.size * 6, transcendentals=0
        ),
        name=f"unpack_{part}",
    )(returns, got, *more)


def local(spectra, library, cand_block, cand_local):
    devices = lax.axis_size("lib")
    num_query, num_bins = spectra.shape
    touches, per_touch = cand_local.shape[1], cand_local.shape[2]
    depth = depth_of(num_query, touches, devices)
    blocks = num_bins // LANES
    me = lax.axis_index("lib").astype(jnp.int32).reshape(1)

    own = cand_block.reshape(-1)
    named = lax.all_gather(
        jnp.concatenate([own, cand_local.reshape(-1)]), "lib", axis=0, tiled=False
    )
    named, wanted = named[:, : own.shape[0]], named[:, own.shape[0] :]
    queries = lax.all_gather(prepare(spectra), "lib", axis=0, tiled=True)
    rows = library.reshape(-1, blocks, LANES)
    slots, returns = route(me, named.reshape(-1), own, num_query, touches, depth)

    out = None
    for part in range(PARTS):
        answer = profile(
            part, depth, touches, devices, slots, wanted.reshape(-1), queries, rows
        )
        answer = answer.reshape(devices, depth // PARTS * per_touch, SHIFTS)
        got = lax.all_to_all(answer, "lib", split_axis=0, concat_axis=0, tiled=True)
        got = got.reshape(-1, per_touch, SHIFTS)
        out = unpack(part, depth, num_query * touches, returns, got, out)
    return out.reshape(num_query, touches * per_touch, SHIFTS)


def solution(mesh):
    placed = (
        P(("groups", "lib"), None),
        P("lib", None),
        P(("groups", "lib"), None),
        P(("groups", "lib"), None, None),
    )
    return jax.shard_map(
        local,
        mesh=mesh,
        in_specs=placed,
        out_specs=P(("groups", "lib"), None, None),
        check_vma=False,
    )
```

time: 555 us -> 261 us (0.47)
  the two profiles are of different devices: /device:TPU:13 before, /device:TPU:0 now
where the time goes in v1:
time: 261 us; the launch traced here: 259 us
  Pallas kernels  174 us (67%)
  blocking collectives  23.3 us (9%)
  waiting for transfers between devices  17.1 us (7%)
  starting transfers between devices  15.6 us (6%)
  local copies, waits for them, and re-layouts  15.2 us (6%)
  between operations  13.6 us (5%)
    pallas_call x3, Pallas kernels, profile(): pl.pallas_call(functools.partial(profile_kernel, part, depth, touches), o...  149 us
    all_gather x1, blocking collectives, local(): lax.all_gather(jnp.concatenate([own, cand_local.reshape(-1)]), 'lib', axi...  23.3 us
    all_to_all x3, starting transfers between devices, local(): got = lax.all_to_all(answer, 'lib', split_axis=0, concat_axis=0, tiled=True)  15.6 us
    all_to_all x3, waiting for transfers between devices, local(): got = lax.all_to_all(answer, 'lib', split_axis=0, concat_axis=0, tiled=True)  15.5 us
    unnamed x25, local copies, waits for them, and re-layouts  14.4 us
    pallas_call x1, Pallas kernels, route(): pl.pallas_call(functools.partial(route_kernel, num_query, touches, depth)...  11.6 us
    pallas_call x3, Pallas kernels, unpack(): pl.pallas_call(functools.partial(unpack_kernel, part, depth), out_shape=j...  11.2 us
  transfers between devices with their start and end apart: 4, of which 2 were waited for; matrix products, arithmetic and copies ran while one was open for 3% of the time, Pallas kernels for 46%

profile of v1, /device:TPU:0, one launch (start us, length us, event | category | flops | bytes accessed | tf_op | source)
XLA Modules:
  0.0 258.7 jit_solution(10369550482805914129)
XLA Ops:
  6.5 0.0 all-gather.4.cloned.1.call-start
  6.5 0.9 copy-done.1
  7.4 1.8 prepare.1
  9.2 0.0 all-gather.4.cloned.1.call-update
  9.3 0.8 copy.10
  10.0 0.1 reshape.42.own_ref
  10.1 0.0 copy-start.8
  10.1 0.8 copy.11
  11.0 0.1 reshape.43
  11.1 23.3 %all-gather.1 = s32[16,1,1152]{2,1,0:T(1,128)S(1)} all-gather(s32[1,1,1152]{2,1,0:T(1,128)S(1)} %reshape.55), channel_id=2, replica_groups=mesh['groups'=2,'lib'=16] {'lib'}, dimensions={0}, use_global_device_ids=true | all-gather | bytes 78336 | tf_op jit(solution)/shard_map/all_gather | solution.py:276
  34.4 5.5 %copy.14 = bf16[64,8,32,128]{3,2,1,0:T(8,128)(2,1)} copy(bf16[64,8,32,128]{3,1,2,0:T(8,128)(2,1)} %bitcast.25) | data formatting | bytes 8388608
  39.9 0.0 copy-done.8
  39.9 0.6 slice_bitcast_fusion.1.named_ref
  40.5 11.6 %route.1 = (s32[193]{0:T(256)}, s32[193]{0:T(256)}) custom-call(s32[1]{0:T(128)} %bitcast.me_ref, s32[2048]{0:T(1024)} %slice_bitcast_fusion.1.named_ref, s32[128]{0:T(128)} %copy-done.8), custom_call_target="tpu_custom_call" | custom-call | tf_op jit(solution)/shard_map/route/pallas_call | solution.py:98
  52.1 1.6 all-gather.4.cloned.1.call-done.query_ref
  53.7 1.6 copy-done.3
  55.3 0.6 copy-done.6
  55.9 50.1 %profile_0.1 = bf16[512,1024]{1,0:T(8,128)(2,1)} custom-call(s32[193]{0:T(256)S(1)} %copy-done.6, s32[16384]{0:T(1024)S(1)} %bitcast.22, bf16[256,32,128]{2,1,0:T(8,128)(2,1)S(1)} %copy-done.3, bf16[512,32,128]{2,1,0:T(8,128)(2,1)} %bitcast.26), custom_call_target="tpu_custom_call" | custom-call | flops 36507222016 | bytes 8388608 | tf_op jit(solution)/shard_map/profile_0/pallas_call | solution.py:196
  106.0 3.7 %all-to-all-start.2 = ((bf16[16,32,1024]{2,1,0:T(8,128)(2,1)}), bf16[16,32,1024]{2,1,0:T(8,128)(2,1)S(1)}, u32[]{:S(2)}, u32[]{:S(2)}) async-start(bf16[16,32,1024]{2,1,0:T(8,128)(2,1)} %bitcast.6), calls=%async_computation.2 | async-start | bytes 2097152 | tf_op jit(solution)/shard_map/all_to_all | solution.py:290
  109.7 1.6 copy-done.4
  111.3 50.1 %profile_1.1 = bf16[512,1024]{1,0:T(8,128)(2,1)} custom-call(s32[193]{0:T(256)S(1)} %copy-done.7, s32[16384]{0:T(1024)S(1)} %bitcast.23, bf16[256,32,128]{2,1,0:T(8,128)(2,1)S(1)} %copy-done.4, bf16[512,32,128]{2,1,0:T(8,128)(2,1)} %bitcast.27), custom_call_target="tpu_custom_call" | custom-call | flops 36507222016 | bytes 8388608 | tf_op jit(solution)/shard_map/profile_1/pallas_call | solution.py:196
  161.4 0.0 all-to-all-done.2
  161.4 6.0 %all-to-all-start.1 = ((bf16[16,32,1024]{2,1,0:T(8,128)(2,1)}), bf16[16,32,1024]{2,1,0:T(8,128)(2,1)S(1)}, u32[]{:S(2)}, u32[]{:S(2)}) async-start(bf16[16,32,1024]{2,1,0:T(8,128)(2,1)} %bitcast.4), calls=%async_computation.1 | async-start | bytes 2097152 | tf_op jit(solution)/shard_map/all_to_all | solution.py:290
  167.4 1.6 copy-done.5
  169.0 49.1 %profile_2.1 = bf16[512,1024]{1,0:T(8,128)(2,1)S(1)} custom-call(s32[193]{0:T(256)S(1)} %copy-done.7, s32[16384]{0:T(1024)S(1)} %bitcast.24, bf16[256,32,128]{2,1,0:T(8,128)(2,1)S(1)} %copy-done.5, bf16[512,32,128]{2,1,0:T(8,128)(2,1)} %bitcast.28), custom_call_target="tpu_custom_call" | custom-call | flops 36507222016 | bytes 8388608 | tf_op jit(solution)/shard_map/profile_2/pallas_call | solution.py:196
  218.1 1.0 copy-done
  219.1 0.0 all-to-all-done.1
  219.1 6.0 %all-to-all-start = ((bf16[16,32,1024]{2,1,0:T(8,128)(2,1)}), bf16[16,32,1024]{2,1,0:T(8,128)(2,1)S(1)}, u32[]{:S(2)}, u32[]{:S(2)}) async-start(bf16[16,32,1024]{2,1,0:T(8,128)(2,1)} %bitcast.21), calls=%async_computation | async-start | bytes 2097152 | tf_op jit(solution)/shard_map/all_to_all | solution.py:290
  225.1 3.7 %unpack_0.1.rest_0_ = f32[128,8,1024]{2,1,0:T(8,128)} custom-call(s32[193]{0:T(256)S(1)} %copy-done.2, bf16[64,8,1024]{2,1,0:T(8,128)(2,1)S(1)} %bitcast.20), custom_call_target="tpu_custom_call" | custom-call | bytes 3145728 | tf_op jit(solution)/shard_map/unpack_0/pallas_call | solution.py:249
  228.8 3.8 %unpack_1.1.rest_0_ = f32[128,8,1024]{2,1,0:T(8,128)} custom-call(s32[193]{0:T(256)S(1)} %copy-done.2, bf16[64,8,1024]{2,1,0:T(8,128)(2,1)S(1)} %bitcast.18, f32[128,8,1024]{2,1,0:T(8,128)} %unpack_0.1.rest_0_), custom_call_target="tpu_custom_call", output_to_operand_aliasing={{}: (2, {})} | custom-call | bytes 3145728 | tf_op jit(solution)/shard_map/unpack_1/pallas_call | solution.py:249
  232.6 15.4 %all-to-all-done = bf16[16,32,1024]{2,1,0:T(8,128)(2,1)S(1)} async-done(((bf16[16,32,1024]{2,1,0:T(8,128)(2,1)}), bf16[16,32,1024]{2,1,0:T(8,128)(2,1)S(1)}, u32[]{:S(2)}, u32[]{:S(2)}) %all-to-all-start) | async-done | bytes 1048608 | tf_op jit(solution)/shard_map/all_to_all | solution.py:290
  248.1 3.7 %unpack_2.1 = f32[128,8,1024]{2,1,0:T(8,128)} custom-call(s32[193]{0:T(256)S(1)} %copy-done.2, bf16[64,8,1024]{2,1,0:T(8,128)(2,1)S(1)} %bitcast.19, f32[128,8,1024]{2,1,0:T(8,128)} %unpack_1.1.rest_0_), custom_call_target="tpu_custom_call", output_to_operand_aliasing={{}: (2, {})} | custom-call | bytes 3145728 | tf_op jit(solution)/shard_map/unpack_2/pallas_call | solution.py:249
  (15 shorter events, 0.1 us)
Async XLA Ops:
  6.5 47.1 %all-gather.4.cloned.1.call-start = ((), (), s32[]{:S(2)}) async-start(), calls=%async_computation.3 | async-start | bytes 2228224 | tf_op jit(solution)/shard_map/all_gather | solution.py:280
  6.5 0.9 copy-start.1
  10.1 29.8 %copy-start.8 = (s32[128]{0:T(128)}, s32[128]{0:T(128)S(1)}, u32[]{:S(2)}) copy-start(s32[128]{0:T(128)S(1)} %reshape.42.own_ref) | copy-start | bytes 1540
  53.7 1.6 copy-start.3
  55.3 0.6 copy-start.6
  55.9 53.8 %copy-start.7 = (s32[193]{0:T(256)S(1)}, s32[193]{0:T(256)}, u32[]{:S(2)}) copy-start(s32[193]{0:T(256)} %get-tuple-element.8.slots_ref) | copy-start | bytes 2320
  106.0 55.4 %all-to-all-start.2 = ((bf16[16,32,1024]{2,1,0:T(8,128)(2,1)}), bf16[16,32,1024]{2,1,0:T(8,128)(2,1)S(1)}, u32[]{:S(2)}, u32[]{:S(2)}) async-start(bf16[16,32,1024]{2,1,0:T(8,128)(2,1)} %bitcast.6), calls=%async_computation.2 | async-start | bytes 2097152 | tf_op jit(solution)/shard_map/all_to_all | solution.py:290
  109.7 1.6 copy-start.4
  161.4 57.7 %all-to-all-start.1 = ((bf16[16,32,1024]{2,1,0:T(8,128)(2,1)}), bf16[16,32,1024]{2,1,0:T(8,128)(2,1)S(1)}, u32[]{:S(2)}, u32[]{:S(2)}) async-start(bf16[16,32,1024]{2,1,0:T(8,128)(2,1)} %bitcast.4), calls=%async_computation.1 | async-start | bytes 2097152 | tf_op jit(solution)/shard_map/all_to_all | solution.py:290
  167.4 1.6 copy-start.5
  169.0 56.1 %copy-start.2 = (s32[193]{0:T(256)S(1)}, s32[193]{0:T(256)}, u32[]{:S(2)}) copy-start(s32[193]{0:T(256)} %get-tuple-element.7.returns_ref) | copy-start | bytes 2320
  218.1 1.0 copy-start
  219.1 29.0 %all-to-all-start = ((bf16[16,32,1024]{2,1,0:T(8,128)(2,1)}), bf16[16,32,1024]{2,1,0:T(8,128)(2,1)S(1)}, u32[]{:S(2)}, u32[]{:S(2)}) async-start(bf16[16,32,1024]{2,1,0:T(8,128)(2,1)} %bitcast.21), calls=%async_computation | async-start | bytes 2097152 | tf_op jit(solution)/shard_map/all_to_all | solution.py:290
Sparse Core Ops, SparseCore 0:
  9.5 44.1 all-gather.3

commit v2 on v1

--- a/solution.py
+++ b/solution.py
@@ -13,6 +13,7 @@
 LANES = 128
 VMEM_LIMIT = 48 * 1024 * 1024
 PARTS = 3
+CHAINS = 4
 
 
 def depth_of(num_query, touches, devices):
@@ -166,22 +167,45 @@
                     tile = pltpu.roll(
                         jnp.where(lane16 < LANES - 16 * a, shifted, before_shifted), 16 * a, 1
                     )
-                right_ref[half, pl.ds((blocks - b) * LANES + 16 * a, 16), :] = tile
+                right_ref[
+                    pl.ds((blocks - b) * LANES + 16 * a, 16), half * LANES : (half + 1) * LANES
+                ] = tile
             before, before_shifted = now, shifted
-
+        return scale
+
+    def part_of_sum(low, high):
         left = jnp.concatenate(
-            [left_ref[half, pl.ds(16 * u, 8 * offsets), :] for u in range(tiles)], axis=1
+            [
+                jnp.concatenate(
+                    [left_ref[half, pl.ds(16 * u, 8 * offsets), :] for u in range(low, high)],
+                    axis=1,
+                )
+                for half in range(2)
+            ],
+            axis=0,
         )
-        product = jnp.dot(left, right_ref[half], preferred_element_type=jnp.float32)
-        return [product[8 * o : 8 * o + 8, :] * scale for o in range(offsets)]
+        right = right_ref[pl.ds(2 * LANES * low, 2 * LANES * (high - low)), :]
+        return jnp.dot(left, right, preferred_element_type=jnp.float32)
+
+    cuts = [tiles * c // CHAINS for c in range(CHAINS + 1)]
 
     @pl.loop(0, part_slots // 2)
     def _(pair):
-        first = one(2 * pair, 0)
-        second = one(2 * pair + 1, 1)
+        scales = [one(2 * pair, 0), one(2 * pair + 1, 1)]
+        product = part_of_sum(cuts[0], cuts[1])
+        for c in range(1, CHAINS):
+            product = product + part_of_sum(cuts[c], cuts[c + 1])
         for o in range(offsets):
+            both = [
+                product[
+                    (half * offsets + o) * 8 : (half * offsets + o + 1) * 8,
+                    half * LANES : (half + 1) * LANES,
+                ]
+                * scales[half]
+                for half in range(2)
+            ]
             out_ref[pl.ds(pl.multiple_of(16 * pair, 16), 16), o * LANES : (o + 1) * LANES] = (
-                jnp.concatenate([first[o], second[o]], axis=0).astype(jnp.bfloat16)
+                jnp.concatenate(both, axis=0).astype(jnp.bfloat16)
             )
 
 
@@ -201,7 +225,7 @@
         scratch_shapes=[
             pltpu.VMEM((2, rows, LANES), jnp.float32),
             pltpu.VMEM((2, (blocks + offsets) * 8, 2 * LANES), jnp.bfloat16),
-            pltpu.VMEM((2, (blocks + 2) * LANES, LANES), jnp.bfloat16),
+            pltpu.VMEM(((blocks + 2) * LANES, 2 * LANES), jnp.bfloat16),
         ],
         compiler_params=pltpu.CompilerParams(vmem_limit_bytes=VMEM_LIMIT),
         cost_estimate=pl.CostEstimate(

time: 261 us -> 249 us (0.954)
  Pallas kernels: 174 us -> 162 us
    pallas_call x3, Pallas kernels: 149 us -> 138 us  [profile(): pl.pallas_call(functools.partial(profile_kernel, part, depth, touches), o...]
  transfers between devices with their start and end apart: 4 -> 4, of which waited for: 2 -> 2; matrix products, arithmetic and copies ran while one was open for 3% -> 3% of each run, Pallas kernels for 46% -> 45%
where the time goes in v2:
time: 249 us; the launch traced here: 247 us
  Pallas kernels  162 us (65%)
  blocking collectives  23.3 us (9%)
  waiting for transfers between devices  17.1 us (7%)
  starting transfers between devices  15.6 us (6%)
  local copies, waits for them, and re-layouts  15.2 us (6%)
  between operations  13.6 us (5%)
    pallas_call x3, Pallas kernels, profile(): pl.pallas_call(functools.partial(profile_kernel, part, depth, touches), o...  138 us
    all_gather x1, blocking collectives, local(): lax.all_gather(jnp.concatenate([own, cand_local.reshape(-1)]), 'lib', axi...  23.3 us
    all_to_all x3, starting transfers between devices, local(): got = lax.all_to_all(answer, 'lib', split_axis=0, concat_axis=0, tiled=True)  15.6 us
    all_to_all x3, waiting for transfers between devices, local(): got = lax.all_to_all(answer, 'lib', split_axis=0, concat_axis=0, tiled=True)  15.5 us
    unnamed x25, local copies, waits for them, and re-layouts  14.4 us
    pallas_call x1, Pallas kernels, route(): pl.pallas_call(functools.partial(route_kernel, num_query, touches, depth)...  11.6 us
    pallas_call x3, Pallas kernels, unpack(): pl.pallas_call(functools.partial(unpack_kernel, part, depth), out_shape=j...  11.2 us
  transfers between devices with their start and end apart: 4, of which 2 were waited for; matrix products, arithmetic and copies ran while one was open for 3% of the time, Pallas kernels for 45%

profile of v2, /device:TPU:0, one launch (start us, length us, event | category | flops | bytes accessed | tf_op | source)
XLA Modules:
  0.0 246.9 jit_solution(15937341560374264217)
XLA Ops:
  6.5 0.0 all-gather.4.cloned.1.call-start
  6.5 0.9 copy-done.1
  7.4 1.8 prepare.1
  9.2 0.0 all-gather.4.cloned.1.call-update
  9.3 0.8 copy.10
  10.0 0.1 reshape.42.own_ref
  10.1 0.0 copy-start.8
  10.1 0.8 copy.11
  11.0 0.1 reshape.43
  11.1 23.3 %all-gather.1 = s32[16,1,1152]{2,1,0:T(1,128)S(1)} all-gather(s32[1,1,1152]{2,1,0:T(1,128)S(1)} %reshape.55), channel_id=2, replica_groups=mesh['groups'=2,'lib'=16] {'lib'}, dimensions={0}, use_global_device_ids=true | all-gather | bytes 78336 | tf_op jit(solution)/shard_map/all_gather | solution.py:300
  34.4 5.5 %copy.14 = bf16[64,8,32,128]{3,2,1,0:T(8,128)(2,1)} copy(bf16[64,8,32,128]{3,1,2,0:T(8,128)(2,1)} %bitcast.25) | data formatting | bytes 8388608
  39.9 0.0 copy-done.8
  39.9 0.6 slice_bitcast_fusion.1.named_ref
  40.5 11.6 %route.1 = (s32[193]{0:T(256)}, s32[193]{0:T(256)}) custom-call(s32[1]{0:T(128)} %bitcast.me_ref, s32[2048]{0:T(1024)} %slice_bitcast_fusion.1.named_ref, s32[128]{0:T(128)} %copy-done.8), custom_call_target="tpu_custom_call" | custom-call | tf_op jit(solution)/shard_map/route/pallas_call | solution.py:99
  52.1 1.6 all-gather.4.cloned.1.call-done.query_ref
  53.7 1.6 copy-done.3
  55.3 0.6 copy-done.6
  55.9 46.2 %profile_0.1 = bf16[512,1024]{1,0:T(8,128)(2,1)} custom-call(s32[193]{0:T(256)S(1)} %copy-done.6, s32[16384]{0:T(1024)S(1)} %bitcast.22, bf16[256,32,128]{2,1,0:T(8,128)(2,1)S(1)} %copy-done.3, bf16[512,32,128]{2,1,0:T(8,128)(2,1)} %bitcast.26), custom_call_target="tpu_custom_call" | custom-call | flops 36507222016 | bytes 8388608 | tf_op jit(solution)/shard_map/profile_0/pallas_call | solution.py:220
  102.1 3.7 %all-to-all-start.2 = ((bf16[16,32,1024]{2,1,0:T(8,128)(2,1)}), bf16[16,32,1024]{2,1,0:T(8,128)(2,1)S(1)}, u32[]{:S(2)}, u32[]{:S(2)}) async-start(bf16[16,32,1024]{2,1,0:T(8,128)(2,1)} %bitcast.6), calls=%async_computation.2 | async-start | bytes 2097152 | tf_op jit(solution)/shard_map/all_to_all | solution.py:314
  105.8 1.6 copy-done.4
  107.3 46.2 %profile_1.1 = bf16[512,1024]{1,0:T(8,128)(2,1)} custom-call(s32[193]{0:T(256)S(1)} %copy-done.7, s32[16384]{0:T(1024)S(1)} %bitcast.23, bf16[256,32,128]{2,1,0:T(8,128)(2,1)S(1)} %copy-done.4, bf16[512,32,128]{2,1,0:T(8,128)(2,1)} %bitcast.27), custom_call_target="tpu_custom_call" | custom-call | flops 36507222016 | bytes 8388608 | tf_op jit(solution)/shard_map/profile_1/pallas_call | solution.py:220
  153.5 0.0 all-to-all-done.2
  153.5 6.0 %all-to-all-start.1 = ((bf16[16,32,1024]{2,1,0:T(8,128)(2,1)}), bf16[16,32,1024]{2,1,0:T(8,128)(2,1)S(1)}, u32[]{:S(2)}, u32[]{:S(2)}) async-start(bf16[16,32,1024]{2,1,0:T(8,128)(2,1)} %bitcast.4), calls=%async_computation.1 | async-start | bytes 2097152 | tf_op jit(solution)/shard_map/all_to_all | solution.py:314
  159.5 1.6 copy-done.5
  161.1 45.2 %profile_2.1 = bf16[512,1024]{1,0:T(8,128)(2,1)S(1)} custom-call(s32[193]{0:T(256)S(1)} %copy-done.7, s32[16384]{0:T(1024)S(1)} %bitcast.24, bf16[256,32,128]{2,1,0:T(8,128)(2,1)S(1)} %copy-done.5, bf16[512,32,128]{2,1,0:T(8,128)(2,1)} %bitcast.28), custom_call_target="tpu_custom_call" | custom-call | flops 36507222016 | bytes 8388608 | tf_op jit(solution)/shard_map/profile_2/pallas_call | solution.py:220
  206.3 1.0 copy-done
  207.3 0.0 all-to-all-done.1
  207.3 6.0 %all-to-all-start = ((bf16[16,32,1024]{2,1,0:T(8,128)(2,1)}), bf16[16,32,1024]{2,1,0:T(8,128)(2,1)S(1)}, u32[]{:S(2)}, u32[]{:S(2)}) async-start(bf16[16,32,1024]{2,1,0:T(8,128)(2,1)} %bitcast.21), calls=%async_computation | async-start | bytes 2097152 | tf_op jit(solution)/shard_map/all_to_all | solution.py:314
  213.3 3.7 %unpack_0.1.rest_0_ = f32[128,8,1024]{2,1,0:T(8,128)} custom-call(s32[193]{0:T(256)S(1)} %copy-done.2, bf16[64,8,1024]{2,1,0:T(8,128)(2,1)S(1)} %bitcast.20), custom_call_target="tpu_custom_call" | custom-call | bytes 3145728 | tf_op jit(solution)/shard_map/unpack_0/pallas_call | solution.py:273
  217.1 3.8 %unpack_1.1.rest_0_ = f32[128,8,1024]{2,1,0:T(8,128)} custom-call(s32[193]{0:T(256)S(1)} %copy-done.2, bf16[64,8,1024]{2,1,0:T(8,128)(2,1)S(1)} %bitcast.18, f32[128,8,1024]{2,1,0:T(8,128)} %unpack_0.1.rest_0_), custom_call_target="tpu_custom_call", output_to_operand_aliasing={{}: (2, {})} | custom-call | bytes 3145728 | tf_op jit(solution)/shard_map/unpack_1/pallas_call | solution.py:273
  220.8 15.4 %all-to-all-done = bf16[16,32,1024]{2,1,0:T(8,128)(2,1)S(1)} async-done(((bf16[16,32,1024]{2,1,0:T(8,128)(2,1)}), bf16[16,32,1024]{2,1,0:T(8,128)(2,1)S(1)}, u32[]{:S(2)}, u32[]{:S(2)}) %all-to-all-start) | async-done | bytes 1048608 | tf_op jit(solution)/shard_map/all_to_all | solution.py:314
  236.3 3.7 %unpack_2.1 = f32[128,8,1024]{2,1,0:T(8,128)} custom-call(s32[193]{0:T(256)S(1)} %copy-done.2, bf16[64,8,1024]{2,1,0:T(8,128)(2,1)S(1)} %bitcast.19, f32[128,8,1024]{2,1,0:T(8,128)} %unpack_1.1.rest_0_), custom_call_target="tpu_custom_call", output_to_operand_aliasing={{}: (2, {})} | custom-call | bytes 3145728 | tf_op jit(solution)/shard_map/unpack_2/pallas_call | solution.py:273
  (15 shorter events, 0.1 us)
Async XLA Ops:
  6.5 47.1 %all-gather.4.cloned.1.call-start = ((), (), s32[]{:S(2)}) async-start(), calls=%async_computation.3 | async-start | bytes 2228224 | tf_op jit(solution)/shard_map/all_gather | solution.py:304
  6.5 0.9 copy-start.1
  10.1 29.8 %copy-start.8 = (s32[128]{0:T(128)}, s32[128]{0:T(128)S(1)}, u32[]{:S(2)}) copy-start(s32[128]{0:T(128)S(1)} %reshape.42.own_ref) | copy-start | bytes 1540
  53.7 1.6 copy-start.3
  55.3 0.6 copy-start.6
  55.9 49.9 %copy-start.7 = (s32[193]{0:T(256)S(1)}, s32[193]{0:T(256)}, u32[]{:S(2)}) copy-start(s32[193]{0:T(256)} %get-tuple-element.8.slots_ref) | copy-start | bytes 2320
  102.1 51.5 %all-to-all-start.2 = ((bf16[16,32,1024]{2,1,0:T(8,128)(2,1)}), bf16[16,32,1024]{2,1,0:T(8,128)(2,1)S(1)}, u32[]{:S(2)}, u32[]{:S(2)}) async-start(bf16[16,32,1024]{2,1,0:T(8,128)(2,1)} %bitcast.6), calls=%async_computation.2 | async-start | bytes 2097152 | tf_op jit(solution)/shard_map/all_to_all | solution.py:314
  105.8 1.6 copy-start.4
  153.5 53.8 %all-to-all-start.1 = ((bf16[16,32,1024]{2,1,0:T(8,128)(2,1)}), bf16[16,32,1024]{2,1,0:T(8,128)(2,1)S(1)}, u32[]{:S(2)}, u32[]{:S(2)}) async-start(bf16[16,32,1024]{2,1,0:T(8,128)(2,1)} %bitcast.4), calls=%async_computation.1 | async-start | bytes 2097152 | tf_op jit(solution)/shard_map/all_to_all | solution.py:314
  159.5 1.6 copy-start.5
  161.1 52.2 %copy-start.2 = (s32[193]{0:T(256)S(1)}, s32[193]{0:T(256)}, u32[]{:S(2)}) copy-start(s32[193]{0:T(256)} %get-tuple-element.7.returns_ref) | copy-start | bytes 2320
  206.3 1.0 copy-start
  207.3 29.0 %all-to-all-start = ((bf16[16,32,1024]{2,1,0:T(8,128)(2,1)}), bf16[16,32,1024]{2,1,0:T(8,128)(2,1)S(1)}, u32[]{:S(2)}, u32[]{:S(2)}) async-start(bf16[16,32,1024]{2,1,0:T(8,128)(2,1)} %bitcast.21), calls=%async_computation | async-start | bytes 2097152 | tf_op jit(solution)/shard_map/all_to_all | solution.py:314
Sparse Core Ops, SparseCore 0:
  9.5 44.1 all-gather.3

commit v3 on v2

--- a/solution.py
+++ b/solution.py
@@ -118,7 +118,6 @@
     tiles = (blocks + 2) // 2
     row = lax.broadcasted_iota(jnp.int32, (8, LANES), 0)
     lane = lax.broadcasted_iota(jnp.int32, (8, LANES), 1)
-    lane16 = lax.broadcasted_iota(jnp.int32, (16, LANES), 1)
 
     cand_ref[...] = jnp.zeros(cand_ref.shape, cand_ref.dtype)
     right_ref[...] = jnp.zeros(right_ref.shape, right_ref.dtype)
@@ -146,30 +145,29 @@
             ].astype(jnp.bfloat16)
 
         spectrum = query_ref[touch // touches].astype(jnp.float32)
-        zero = jnp.zeros((8, LANES), jnp.float32)
-        before = (zero, zero)
-        before_shifted = jnp.zeros((16, LANES), jnp.bfloat16)
+        before = before_shifted = jnp.zeros((8, LANES), jnp.float32)
         for b in range(blocks + 1):
             if b < blocks:
                 wide = jnp.broadcast_to(spectrum[b : b + 1, :], (8, LANES))
-                now = tuple(
-                    pltpu.roll(wide, 1 + 8 * h, 1, stride=1, stride_axis=0) for h in range(2)
+                now = pltpu.roll(wide, 1, 1, stride=1, stride_axis=0)
+            else:
+                now = jnp.zeros((8, LANES), jnp.float32)
+            shifted = jnp.where(lane > row, now, before)
+            for a in range(0, LANES, 16):
+                tile = jnp.concatenate(
+                    [
+                        pltpu.roll(
+                            jnp.where(lane < LANES - c, shifted, before_shifted), c, 1
+                        )
+                        if c
+                        else shifted
+                        for c in (a, a + 8)
+                    ],
+                    axis=0,
                 )
-            else:
-                now = (zero, zero)
-            shifted = jnp.concatenate(
-                [jnp.where(lane > row + 8 * h, now[h], before[h]) for h in range(2)], axis=0
-            ).astype(jnp.bfloat16)
-            for a in range(8):
-                if a == 0:
-                    tile = shifted
-                else:
-                    tile = pltpu.roll(
-                        jnp.where(lane16 < LANES - 16 * a, shifted, before_shifted), 16 * a, 1
-                    )
                 right_ref[
-                    pl.ds((blocks - b) * LANES + 16 * a, 16), half * LANES : (half + 1) * LANES
-                ] = tile
+                    pl.ds((blocks - b) * LANES + a, 16), half * LANES : (half + 1) * LANES
+                ] = tile.astype(jnp.bfloat16)
             before, before_shifted = now, shifted
         return scale
 

time: 249 us -> 336 us (1.35)
  Pallas kernels: 162 us -> 250 us
    pallas_call x3, Pallas kernels: 138 us -> 225 us  [profile(): pl.pallas_call(functools.partial(profile_kernel, part, depth, touches), o...]
  transfers between devices with their start and end apart: 4 -> 4, of which waited for: 2 -> 2; matrix products, arithmetic and copies ran while one was open for 3% -> 2% of each run, Pallas kernels for 45% -> 50%
where the time goes in v3:
time: 336 us; the launch traced here: 334 us
  Pallas kernels  250 us (74%)
  blocking collectives  23.3 us (7%)
  waiting for transfers between devices  17.1 us (5%)
  starting transfers between devices  15.6 us (5%)
  local copies, waits for them, and re-layouts  15.2 us (5%)
  between operations  13.6 us (4%)
    pallas_call x3, Pallas kernels, profile(): pl.pallas_call(functools.partial(profile_kernel, part, depth, touches), o...  225 us
    all_gather x1, blocking collectives, local(): lax.all_gather(jnp.concatenate([own, cand_local.reshape(-1)]), 'lib', axi...  23.3 us
    all_to_all x3, starting transfers between devices, local(): got = lax.all_to_all(answer, 'lib', split_axis=0, concat_axis=0, tiled=True)  15.6 us
    all_to_all x3, waiting for transfers between devices, local(): got = lax.all_to_all(answer, 'lib', split_axis=0, concat_axis=0, tiled=True)  15.5 us
    unnamed x25, local copies, waits for them, and re-layouts  14.4 us
    pallas_call x1, Pallas kernels, route(): pl.pallas_call(functools.partial(route_kernel, num_query, touches, depth)...  11.6 us
    pallas_call x3, Pallas kernels, unpack(): pl.pallas_call(functools.partial(unpack_kernel, part, depth), out_shape=j...  11.2 us
  transfers between devices with their start and end apart: 4, of which 2 were waited for; matrix products, arithmetic and copies ran while one was open for 2% of the time, Pallas kernels for 50%

profile of v3, /device:TPU:0, one launch (start us, length us, event | category | flops | bytes accessed | tf_op | source)
XLA Modules:
  0.0 334.4 jit_solution(1676781623202222320)
XLA Ops:
  6.5 0.0 all-gather.4.cloned.1.call-start
  6.5 0.9 copy-done.1
  7.4 1.8 prepare.1
  9.2 0.0 all-gather.4.cloned.1.call-update
  9.3 0.8 copy.10
  10.0 0.1 reshape.42.own_ref
  10.1 0.0 copy-start.8
  10.1 0.8 copy.11
  11.0 0.1 reshape.43
  11.1 23.3 %all-gather.1 = s32[16,1,1152]{2,1,0:T(1,128)S(1)} all-gather(s32[1,1,1152]{2,1,0:T(1,128)S(1)} %reshape.55), channel_id=2, replica_groups=mesh['groups'=2,'lib'=16] {'lib'}, dimensions={0}, use_global_device_ids=true | all-gather | bytes 78336 | tf_op jit(solution)/shard_map/all_gather | solution.py:298
  34.4 5.5 %copy.14 = bf16[64,8,32,128]{3,2,1,0:T(8,128)(2,1)} copy(bf16[64,8,32,128]{3,1,2,0:T(8,128)(2,1)} %bitcast.25) | data formatting | bytes 8388608
  39.9 0.6 slice_bitcast_fusion.1.named_ref
  40.5 11.6 %route.1 = (s32[193]{0:T(256)}, s32[193]{0:T(256)}) custom-call(s32[1]{0:T(128)} %bitcast.me_ref, s32[2048]{0:T(1024)} %slice_bitcast_fusion.1.named_ref, s32[128]{0:T(128)} %copy-done.8), custom_call_target="tpu_custom_call" | custom-call | tf_op jit(solution)/shard_map/route/pallas_call | solution.py:99
  52.1 1.6 all-gather.4.cloned.1.call-done.query_ref
  53.7 1.6 copy-done.3
  55.3 0.6 copy-done.6
  55.9 75.3 %profile_0.1 = bf16[512,1024]{1,0:T(8,128)(2,1)} custom-call(s32[193]{0:T(256)S(1)} %copy-done.6, s32[16384]{0:T(1024)S(1)} %bitcast.22, bf16[256,32,128]{2,1,0:T(8,128)(2,1)S(1)} %copy-done.3, bf16[512,32,128]{2,1,0:T(8,128)(2,1)} %bitcast.26), custom_call_target="tpu_custom_call" | custom-call | flops 36507222016 | bytes 8388608 | tf_op jit(solution)/shard_map/profile_0/pallas_call | solution.py:218
  131.2 3.7 %all-to-all-start.2 = ((bf16[16,32,1024]{2,1,0:T(8,128)(2,1)}), bf16[16,32,1024]{2,1,0:T(8,128)(2,1)S(1)}, u32[]{:S(2)}, u32[]{:S(2)}) async-start(bf16[16,32,1024]{2,1,0:T(8,128)(2,1)} %bitcast.6), calls=%async_computation.2 | async-start | bytes 2097152 | tf_op jit(solution)/shard_map/all_to_all | solution.py:312
  134.9 1.6 copy-done.4
  136.5 75.4 %profile_1.1 = bf16[512,1024]{1,0:T(8,128)(2,1)} custom-call(s32[193]{0:T(256)S(1)} %copy-done.7, s32[16384]{0:T(1024)S(1)} %bitcast.23, bf16[256,32,128]{2,1,0:T(8,128)(2,1)S(1)} %copy-done.4, bf16[512,32,128]{2,1,0:T(8,128)(2,1)} %bitcast.27), custom_call_target="tpu_custom_call" | custom-call | flops 36507222016 | bytes 8388608 | tf_op jit(solution)/shard_map/profile_1/pallas_call | solution.py:218
  211.9 0.0 all-to-all-done.2
  211.9 6.0 %all-to-all-start.1 = ((bf16[16,32,1024]{2,1,0:T(8,128)(2,1)}), bf16[16,32,1024]{2,1,0:T(8,128)(2,1)S(1)}, u32[]{:S(2)}, u32[]{:S(2)}) async-start(bf16[16,32,1024]{2,1,0:T(8,128)(2,1)} %bitcast.4), calls=%async_computation.1 | async-start | bytes 2097152 | tf_op jit(solution)/shard_map/all_to_all | solution.py:312
  217.9 0.0 copy-start.5
  217.9 1.6 copy-done.5
  219.4 74.4 %profile_2.1 = bf16[512,1024]{1,0:T(8,128)(2,1)S(1)} custom-call(s32[193]{0:T(256)S(1)} %copy-done.7, s32[16384]{0:T(1024)S(1)} %bitcast.24, bf16[256,32,128]{2,1,0:T(8,128)(2,1)S(1)} %copy-done.5, bf16[512,32,128]{2,1,0:T(8,128)(2,1)} %bitcast.28), custom_call_target="tpu_custom_call" | custom-call | flops 36507222016 | bytes 8388608 | tf_op jit(solution)/shard_map/profile_2/pallas_call | solution.py:218
  293.8 1.0 copy-done
  294.8 0.0 all-to-all-done.1
  294.8 6.0 %all-to-all-start = ((bf16[16,32,1024]{2,1,0:T(8,128)(2,1)}), bf16[16,32,1024]{2,1,0:T(8,128)(2,1)S(1)}, u32[]{:S(2)}, u32[]{:S(2)}) async-start(bf16[16,32,1024]{2,1,0:T(8,128)(2,1)} %bitcast.21), calls=%async_computation | async-start | bytes 2097152 | tf_op jit(solution)/shard_map/all_to_all | solution.py:312
  300.8 3.7 %unpack_0.1.rest_0_ = f32[128,8,1024]{2,1,0:T(8,128)} custom-call(s32[193]{0:T(256)S(1)} %copy-done.2, bf16[64,8,1024]{2,1,0:T(8,128)(2,1)S(1)} %bitcast.20), custom_call_target="tpu_custom_call" | custom-call | bytes 3145728 | tf_op jit(solution)/shard_map/unpack_0/pallas_call | solution.py:271
  304.6 3.8 %unpack_1.1.rest_0_ = f32[128,8,1024]{2,1,0:T(8,128)} custom-call(s32[193]{0:T(256)S(1)} %copy-done.2, bf16[64,8,1024]{2,1,0:T(8,128)(2,1)S(1)} %bitcast.18, f32[128,8,1024]{2,1,0:T(8,128)} %unpack_0.1.rest_0_), custom_call_target="tpu_custom_call", output_to_operand_aliasing={{}: (2, {})} | custom-call | bytes 3145728 | tf_op jit(solution)/shard_map/unpack_1/pallas_call | solution.py:271
  308.3 15.4 %all-to-all-done = bf16[16,32,1024]{2,1,0:T(8,128)(2,1)S(1)} async-done(((bf16[16,32,1024]{2,1,0:T(8,128)(2,1)}), bf16[16,32,1024]{2,1,0:T(8,128)(2,1)S(1)}, u32[]{:S(2)}, u32[]{:S(2)}) %all-to-all-start) | async-done | bytes 1048608 | tf_op jit(solution)/shard_map/all_to_all | solution.py:312
  323.8 3.7 %unpack_2.1 = f32[128,8,1024]{2,1,0:T(8,128)} custom-call(s32[193]{0:T(256)S(1)} %copy-done.2, bf16[64,8,1024]{2,1,0:T(8,128)(2,1)S(1)} %bitcast.19, f32[128,8,1024]{2,1,0:T(8,128)} %unpack_1.1.rest_0_), custom_call_target="tpu_custom_call", output_to_operand_aliasing={{}: (2, {})} | custom-call | bytes 3145728 | tf_op jit(solution)/shard_map/unpack_2/pallas_call | solution.py:271
  (15 shorter events, 0.1 us)
Async XLA Ops:
  6.5 47.1 %all-gather.4.cloned.1.call-start = ((), (), s32[]{:S(2)}) async-start(), calls=%async_computation.3 | async-start | bytes 2228224 | tf_op jit(solution)/shard_map/all_gather | solution.py:302
  6.5 0.9 copy-start.1
  10.1 29.8 %copy-start.8 = (s32[128]{0:T(128)}, s32[128]{0:T(128)S(1)}, u32[]{:S(2)}) copy-start(s32[128]{0:T(128)S(1)} %reshape.42.own_ref) | copy-start | bytes 1540
  53.7 1.6 copy-start.3
  55.3 0.6 copy-start.6
  55.9 79.0 %copy-start.7 = (s32[193]{0:T(256)S(1)}, s32[193]{0:T(256)}, u32[]{:S(2)}) copy-start(s32[193]{0:T(256)} %get-tuple-element.8.slots_ref) | copy-start | bytes 2320
  131.2 80.6 %all-to-all-start.2 = ((bf16[16,32,1024]{2,1,0:T(8,128)(2,1)}), bf16[16,32,1024]{2,1,0:T(8,128)(2,1)S(1)}, u32[]{:S(2)}, u32[]{:S(2)}) async-start(bf16[16,32,1024]{2,1,0:T(8,128)(2,1)} %bitcast.6), calls=%async_computation.2 | async-start | bytes 2097152 | tf_op jit(solution)/shard_map/all_to_all | solution.py:312
  134.9 1.6 copy-start.4
  211.9 83.0 %all-to-all-start.1 = ((bf16[16,32,1024]{2,1,0:T(8,128)(2,1)}), bf16[16,32,1024]{2,1,0:T(8,128)(2,1)S(1)}, u32[]{:S(2)}, u32[]{:S(2)}) async-start(bf16[16,32,1024]{2,1,0:T(8,128)(2,1)} %bitcast.4), calls=%async_computation.1 | async-start | bytes 2097152 | tf_op jit(solution)/shard_map/all_to_all | solution.py:312
  217.9 1.6 copy-start.5
  219.4 81.4 %copy-start.2 = (s32[193]{0:T(256)S(1)}, s32[193]{0:T(256)}, u32[]{:S(2)}) copy-start(s32[193]{0:T(256)} %get-tuple-element.7.returns_ref) | copy-start | bytes 2320
  293.8 1.0 copy-start
  294.8 29.0 %all-to-all-start = ((bf16[16,32,1024]{2,1,0:T(8,128)(2,1)}), bf16[16,32,1024]{2,1,0:T(8,128)(2,1)S(1)}, u32[]{:S(2)}, u32[]{:S(2)}) async-start(bf16[16,32,1024]{2,1,0:T(8,128)(2,1)} %bitcast.21), calls=%async_computation | async-start | bytes 2097152 | tf_op jit(solution)/shard_map/all_to_all | solution.py:312
Sparse Core Ops, SparseCore 0:
  9.5 44.1 all-gather.3

commit v4 on v1

--- a/solution.py
+++ b/solution.py
@@ -13,6 +13,9 @@
 LANES = 128
 VMEM_LIMIT = 48 * 1024 * 1024
 PARTS = 3
+CHAINS = 2
+GROUPS = 4
+WIDTH = LANES // GROUPS
 
 
 def depth_of(num_query, touches, devices):
@@ -106,51 +109,69 @@
 
 def profile_kernel(
     part, depth, touches, slots_ref, local_ref, query_ref, library_ref, out_ref,
-    cand_ref, left_ref, right_ref,
+    cand_ref, spectrum_ref, left_ref, right_ref,
 ):
     per_touch = 8
+    rows = 2 * per_touch
     blocks = query_ref.shape[1]
     offsets = SHIFTS // LANES
-    edge = offsets // 2
+    first = offsets // 2 + 1
     part_depth = depth // PARTS
     part_slots = out_ref.shape[0] // per_touch
-    tiles = (blocks + 2) // 2
+    tiles = blocks // GROUPS
     row = lax.broadcasted_iota(jnp.int32, (8, LANES), 0)
     lane = lax.broadcasted_iota(jnp.int32, (8, LANES), 1)
-    lane16 = lax.broadcasted_iota(jnp.int32, (16, LANES), 1)
+    lane16 = lax.broadcasted_iota(jnp.int32, (rows, LANES), 1)
 
     cand_ref[...] = jnp.zeros(cand_ref.shape, cand_ref.dtype)
     right_ref[...] = jnp.zeros(right_ref.shape, right_ref.dtype)
 
-    def one(slot, half):
+    def choose(pieces):
+        value = pieces[0]
+        for group in range(1, GROUPS):
+            value = jnp.where(lane16 < group * WIDTH, value, pieces[group])
+        return value
+
+    def gather(slot, half):
         place = slot // part_depth * depth + part * part_depth + slot % part_depth
         touch = jnp.maximum(slots_ref[place], 0)
-        square = jnp.zeros((per_touch, LANES), jnp.float32)
         for k in range(per_touch):
             wanted = local_ref[touch * per_touch + k]
-            cand_ref[half, pl.ds(edge * per_touch + k, blocks, stride=per_touch), :] = (
+            cand_ref[pl.ds(first * rows + half * per_touch + k, blocks, stride=rows), :] = (
                 library_ref[wanted].astype(jnp.float32)
             )
+        square = jnp.zeros((per_touch, LANES), jnp.float32)
         for b in range(blocks):
-            piece = cand_ref[half, pl.ds((edge + b) * per_touch, per_touch), :]
+            piece = cand_ref[pl.ds((first + b) * rows + half * per_touch, per_touch), :]
             square = square + piece * piece
         mean = jnp.sum(square, axis=1, keepdims=True) / (blocks * LANES)
-        scale = lax.rsqrt(mean + EPSILON)
-        for g in range((blocks + offsets) // 2):
-            left_ref[half, pl.ds(16 * g, 16), 0:LANES] = cand_ref[
-                half, pl.ds(16 * g, 16), :
-            ].astype(jnp.bfloat16)
-            left_ref[half, pl.ds(16 * g, 16), LANES : 2 * LANES] = cand_ref[
-                half, pl.ds(16 * g + 8, 16), :
-            ].astype(jnp.bfloat16)
-
-        spectrum = query_ref[touch // touches].astype(jnp.float32)
+        return touch // touches, lax.rsqrt(mean + EPSILON)
+
+    def make_left():
+        pieces = [
+            cand_ref[pl.ds(rows * b, rows), :].astype(jnp.bfloat16)
+            for b in range(blocks + offsets + 1)
+        ]
+        for t in range(tiles + offsets + 1):
+            given = [pieces[t + tiles * g] for g in range(GROUPS)]
+            turned = []
+            for c in range(GROUPS):
+                mixed = choose([given[(a + c) % GROUPS] for a in range(GROUPS)])
+                turned.append(pltpu.roll(mixed, WIDTH * c, 1) if c else mixed)
+            for a in range(GROUPS):
+                left_ref[a, pl.ds(rows * t, rows), :] = choose(
+                    [turned[(g - a) % GROUPS] for g in range(GROUPS)]
+                )
+
+    def make_right(query, half):
+        spectrum_ref[half] = query_ref[query].astype(jnp.float32)
         zero = jnp.zeros((8, LANES), jnp.float32)
         before = (zero, zero)
         before_shifted = jnp.zeros((16, LANES), jnp.bfloat16)
+        columns = slice(half * LANES, (half + 1) * LANES)
         for b in range(blocks + 1):
             if b < blocks:
-                wide = jnp.broadcast_to(spectrum[b : b + 1, :], (8, LANES))
+                wide = jnp.broadcast_to(spectrum_ref[half, pl.ds(b, 1), :], (8, LANES))
                 now = tuple(
                     pltpu.roll(wide, 1 + 8 * h, 1, stride=1, stride_axis=0) for h in range(2)
                 )
@@ -159,29 +180,60 @@
             shifted = jnp.concatenate(
                 [jnp.where(lane > row + 8 * h, now[h], before[h]) for h in range(2)], axis=0
             ).astype(jnp.bfloat16)
-            for a in range(8):
-                if a == 0:
-                    tile = shifted
-                else:
-                    tile = pltpu.roll(
-                        jnp.where(lane16 < LANES - 16 * a, shifted, before_shifted), 16 * a, 1
-                    )
-                right_ref[half, pl.ds((blocks - b) * LANES + 16 * a, 16), :] = tile
+            j = blocks - 1 - b
+            place = 0 if j < 0 else (j % tiles + 1) * LANES + j // tiles * WIDTH
+            right_ref[pl.ds(place, 16), columns] = shifted
+            for c in range(16, WIDTH, 16):
+                right_ref[pl.ds(place + c, 16), columns] = pltpu.roll(
+                    jnp.where(lane16 < LANES - c, shifted, before_shifted), c, 1
+                )
             before, before_shifted = now, shifted
 
+    def sums(low, high):
         left = jnp.concatenate(
-            [left_ref[half, pl.ds(16 * u, 8 * offsets), :] for u in range(tiles)], axis=1
+            [
+                jnp.concatenate(
+                    [
+                        left_ref[a, pl.ds(rows * t, rows * (offsets + 1)), :]
+                        for t in range(tiles + 1)
+                    ],
+                    axis=1,
+                )
+                for a in range(low, high)
+            ],
+            axis=0,
         )
-        product = jnp.dot(left, right_ref[half], preferred_element_type=jnp.float32)
-        return [product[8 * o : 8 * o + 8, :] * scale for o in range(offsets)]
+        return jnp.dot(left, right_ref[...], preferred_element_type=jnp.float32)
 
     @pl.loop(0, part_slots // 2)
     def _(pair):
-        first = one(2 * pair, 0)
-        second = one(2 * pair + 1, 1)
+        queries, scales = zip(*[gather(2 * pair + half, half) for half in range(2)])
+        make_left()
+        for half in range(2):
+            make_right(queries[half], half)
+        step = GROUPS // CHAINS
+        products = [sums(step * c, step * (c + 1)) for c in range(CHAINS)]
+
+        def found(a, o, half):
+            at = ((a % step) * (offsets + 1) + o) * rows + half * per_touch
+            return products[a // step][at : at + per_touch, half * LANES : (half + 1) * LANES]
+
         for o in range(offsets):
+            both = []
+            for half in range(2):
+                total = found(0, o + 1, half)
+                for a in range(1, GROUPS):
+                    shift = WIDTH * a
+                    total = total + pltpu.roll(
+                        jnp.where(
+                            lane < LANES - shift, found(a, o + 1, half), found(a, o, half)
+                        ),
+                        shift,
+                        1,
+                    )
+                both.append(total * scales[half])
             out_ref[pl.ds(pl.multiple_of(16 * pair, 16), 16), o * LANES : (o + 1) * LANES] = (
-                jnp.concatenate([first[o], second[o]], axis=0).astype(jnp.bfloat16)
+                jnp.concatenate(both, axis=0).astype(jnp.bfloat16)
             )
 
 
@@ -189,19 +241,20 @@
     blocks = queries.shape[1]
     offsets = SHIFTS // LANES
     part_slots = devices * depth // PARTS
-    rows = (blocks + offsets + 2) * 8
+    tiles = blocks // GROUPS
     smem = pl.BlockSpec(memory_space=pltpu.SMEM)
     vmem = pl.BlockSpec(memory_space=pltpu.VMEM)
-    flops = part_slots * 2 * 8 * offsets * (blocks + 2) * LANES * LANES
+    flops = part_slots * 2 * 8 * (offsets + 1) * (blocks + 4) * LANES * LANES
     return pl.pallas_call(
         functools.partial(profile_kernel, part, depth, touches),
         out_shape=jax.ShapeDtypeStruct((part_slots * 8, SHIFTS), jnp.bfloat16),
         in_specs=[smem, smem, vmem, vmem],
         out_specs=vmem,
         scratch_shapes=[
-            pltpu.VMEM((2, rows, LANES), jnp.float32),
-            pltpu.VMEM((2, (blocks + offsets) * 8, 2 * LANES), jnp.bfloat16),
-            pltpu.VMEM((2, (blocks + 2) * LANES, LANES), jnp.bfloat16),
+            pltpu.VMEM(((blocks + offsets + 1) * 16, LANES), jnp.float32),
+            pltpu.VMEM((2, blocks, LANES), jnp.float32),
+            pltpu.VMEM((GROUPS, (tiles + offsets + 1) * 16, LANES), jnp.bfloat16),
+            pltpu.VMEM(((tiles + 1) * LANES, 2 * LANES), jnp.bfloat16),
         ],
         compiler_params=pltpu.CompilerParams(vmem_limit_bytes=VMEM_LIMIT),
         cost_estimate=pl.CostEstimate(

time: 261 us -> 221 us (0.85)
  Pallas kernels: 174 us -> 134 us
    pallas_call x3, Pallas kernels: 149 us -> 109 us  [profile(): pl.pallas_call(functools.partial(profile_kernel, part, depth, touches), o...]
  transfers between devices with their start and end apart: 4 -> 4, of which waited for: 2 -> 2; matrix products, arithmetic and copies ran while one was open for 3% -> 4% of each run, Pallas kernels for 46% -> 42%
where the time goes in v4:
time: 221 us; the launch traced here: 219 us
  Pallas kernels  134 us (61%)
  blocking collectives  23.3 us (11%)
  waiting for transfers between devices  17.1 us (8%)
  starting transfers between devices  15.6 us (7%)
  local copies, waits for them, and re-layouts  15.2 us (7%)
  between operations  13.6 us (6%)
    pallas_call x3, Pallas kernels, profile(): pl.pallas_call(functools.partial(profile_kernel, part, depth, touches), o...  109 us
    all_gather x1, blocking collectives, local(): lax.all_gather(jnp.concatenate([own, cand_local.reshape(-1)]), 'lib', axi...  23.3 us
    all_to_all x3, starting transfers between devices, local(): got = lax.all_to_all(answer, 'lib', split_axis=0, concat_axis=0, tiled=True)  15.6 us
    all_to_all x3, waiting for transfers between devices, local(): got = lax.all_to_all(answer, 'lib', split_axis=0, concat_axis=0, tiled=True)  15.5 us
    unnamed x25, local copies, waits for them, and re-layouts  14.4 us
    pallas_call x1, Pallas kernels, route(): pl.pallas_call(functools.partial(route_kernel, num_query, touches, depth)...  11.6 us
    pallas_call x3, Pallas kernels, unpack(): pl.pallas_call(functools.partial(unpack_kernel, part, depth), out_shape=j...  11.2 us
  transfers between devices with their start and end apart: 4, of which 2 were waited for; matrix products, arithmetic and copies ran while one was open for 4% of the time, Pallas kernels for 42%

profile of v4, /device:TPU:0, one launch (start us, length us, event | category | flops | bytes accessed | tf_op | source)
XLA Modules:
  0.0 218.7 jit_solution(7576286622549356369)
XLA Ops:
  6.5 0.0 all-gather.4.cloned.1.call-start
  6.5 0.9 copy-done.1
  7.4 1.8 prepare.1
  9.2 0.0 all-gather.4.cloned.1.call-update
  9.3 0.8 copy.10
  10.0 0.1 reshape.42.own_ref
  10.1 0.8 copy.11
  11.0 0.1 reshape.43
  11.1 23.3 %all-gather.1 = s32[16,1,1152]{2,1,0:T(1,128)S(1)} all-gather(s32[1,1,1152]{2,1,0:T(1,128)S(1)} %reshape.55), channel_id=2, replica_groups=mesh['groups'=2,'lib'=16] {'lib'}, dimensions={0}, use_global_device_ids=true | all-gather | bytes 78336 | tf_op jit(solution)/shard_map/all_gather | solution.py:329
  34.4 5.5 %copy.14 = bf16[64,8,32,128]{3,2,1,0:T(8,128)(2,1)} copy(bf16[64,8,32,128]{3,1,2,0:T(8,128)(2,1)} %bitcast.25) | data formatting | bytes 8388608
  39.9 0.0 copy-done.8
  39.9 0.6 slice_bitcast_fusion.1.named_ref
  40.5 11.6 %route.1 = (s32[193]{0:T(256)}, s32[193]{0:T(256)}) custom-call(s32[1]{0:T(128)} %bitcast.me_ref, s32[2048]{0:T(1024)} %slice_bitcast_fusion.1.named_ref, s32[128]{0:T(128)} %copy-done.8), custom_call_target="tpu_custom_call" | custom-call | tf_op jit(solution)/shard_map/route/pallas_call | solution.py:101
  52.1 1.6 all-gather.4.cloned.1.call-done.query_ref
  53.7 1.6 copy-done.3
  55.3 0.6 copy-done.6
  55.9 36.8 %profile_0.1 = bf16[512,1024]{1,0:T(8,128)(2,1)} custom-call(s32[193]{0:T(256)S(1)} %copy-done.6, s32[16384]{0:T(1024)S(1)} %bitcast.22, bf16[256,32,128]{2,1,0:T(8,128)(2,1)S(1)} %copy-done.3, bf16[512,32,128]{2,1,0:T(8,128)(2,1)} %bitcast.26), custom_call_target="tpu_custom_call" | custom-call | flops 43486543872 | bytes 8388608 | tf_op jit(solution)/shard_map/profile_0/pallas_call | solution.py:248
  92.7 3.7 %all-to-all-start.2 = ((bf16[16,32,1024]{2,1,0:T(8,128)(2,1)}), bf16[16,32,1024]{2,1,0:T(8,128)(2,1)S(1)}, u32[]{:S(2)}, u32[]{:S(2)}) async-start(bf16[16,32,1024]{2,1,0:T(8,128)(2,1)} %bitcast.6), calls=%async_computation.2 | async-start | bytes 2097152 | tf_op jit(solution)/shard_map/all_to_all | solution.py:343
  96.4 0.0 copy-done.7
  96.4 1.6 copy-done.4
  98.0 36.8 %profile_1.1 = bf16[512,1024]{1,0:T(8,128)(2,1)} custom-call(s32[193]{0:T(256)S(1)} %copy-done.7, s32[16384]{0:T(1024)S(1)} %bitcast.23, bf16[256,32,128]{2,1,0:T(8,128)(2,1)S(1)} %copy-done.4, bf16[512,32,128]{2,1,0:T(8,128)(2,1)} %bitcast.27), custom_call_target="tpu_custom_call" | custom-call | flops 43486543872 | bytes 8388608 | tf_op jit(solution)/shard_map/profile_1/pallas_call | solution.py:248
  134.8 0.0 all-to-all-done.2
  134.8 6.0 %all-to-all-start.1 = ((bf16[16,32,1024]{2,1,0:T(8,128)(2,1)}), bf16[16,32,1024]{2,1,0:T(8,128)(2,1)S(1)}, u32[]{:S(2)}, u32[]{:S(2)}) async-start(bf16[16,32,1024]{2,1,0:T(8,128)(2,1)} %bitcast.4), calls=%async_computation.1 | async-start | bytes 2097152 | tf_op jit(solution)/shard_map/all_to_all | solution.py:343
  140.7 1.6 copy-done.5
  142.3 35.8 %profile_2.1 = bf16[512,1024]{1,0:T(8,128)(2,1)S(1)} custom-call(s32[193]{0:T(256)S(1)} %copy-done.7, s32[16384]{0:T(1024)S(1)} %bitcast.24, bf16[256,32,128]{2,1,0:T(8,128)(2,1)S(1)} %copy-done.5, bf16[512,32,128]{2,1,0:T(8,128)(2,1)} %bitcast.28), custom_call_target="tpu_custom_call" | custom-call | flops 43486543872 | bytes 8388608 | tf_op jit(solution)/shard_map/profile_2/pallas_call | solution.py:248
  178.2 1.0 copy-done
  179.1 0.0 all-to-all-done.1
  179.1 6.0 %all-to-all-start = ((bf16[16,32,1024]{2,1,0:T(8,128)(2,1)}), bf16[16,32,1024]{2,1,0:T(8,128)(2,1)S(1)}, u32[]{:S(2)}, u32[]{:S(2)}) async-start(bf16[16,32,1024]{2,1,0:T(8,128)(2,1)} %bitcast.21), calls=%async_computation | async-start | bytes 2097152 | tf_op jit(solution)/shard_map/all_to_all | solution.py:343
  185.2 3.7 %unpack_0.1.rest_0_ = f32[128,8,1024]{2,1,0:T(8,128)} custom-call(s32[193]{0:T(256)S(1)} %copy-done.2, bf16[64,8,1024]{2,1,0:T(8,128)(2,1)S(1)} %bitcast.20), custom_call_target="tpu_custom_call" | custom-call | bytes 3145728 | tf_op jit(solution)/shard_map/unpack_0/pallas_call | solution.py:302
  188.9 3.8 %unpack_1.1.rest_0_ = f32[128,8,1024]{2,1,0:T(8,128)} custom-call(s32[193]{0:T(256)S(1)} %copy-done.2, bf16[64,8,1024]{2,1,0:T(8,128)(2,1)S(1)} %bitcast.18, f32[128,8,1024]{2,1,0:T(8,128)} %unpack_0.1.rest_0_), custom_call_target="tpu_custom_call", output_to_operand_aliasing={{}: (2, {})} | custom-call | bytes 3145728 | tf_op jit(solution)/shard_map/unpack_1/pallas_call | solution.py:302
  192.6 15.4 %all-to-all-done = bf16[16,32,1024]{2,1,0:T(8,128)(2,1)S(1)} async-done(((bf16[16,32,1024]{2,1,0:T(8,128)(2,1)}), bf16[16,32,1024]{2,1,0:T(8,128)(2,1)S(1)}, u32[]{:S(2)}, u32[]{:S(2)}) %all-to-all-start) | async-done | bytes 1048608 | tf_op jit(solution)/shard_map/all_to_all | solution.py:343
  208.1 3.7 %unpack_2.1 = f32[128,8,1024]{2,1,0:T(8,128)} custom-call(s32[193]{0:T(256)S(1)} %copy-done.2, bf16[64,8,1024]{2,1,0:T(8,128)(2,1)S(1)} %bitcast.19, f32[128,8,1024]{2,1,0:T(8,128)} %unpack_1.1.rest_0_), custom_call_target="tpu_custom_call", output_to_operand_aliasing={{}: (2, {})} | custom-call | bytes 3145728 | tf_op jit(solution)/shard_map/unpack_2/pallas_call | solution.py:302
  (15 shorter events, 0.1 us)
Async XLA Ops:
  6.5 47.1 %all-gather.4.cloned.1.call-start = ((), (), s32[]{:S(2)}) async-start(), calls=%async_computation.3 | async-start | bytes 2228224 | tf_op jit(solution)/shard_map/all_gather | solution.py:333
  6.5 0.9 copy-start.1
  10.1 29.8 %copy-start.8 = (s32[128]{0:T(128)}, s32[128]{0:T(128)S(1)}, u32[]{:S(2)}) copy-start(s32[128]{0:T(128)S(1)} %reshape.42.own_ref) | copy-start | bytes 1540
  53.7 1.6 copy-start.3
  55.3 0.6 copy-start.6
  55.9 40.5 %copy-start.7 = (s32[193]{0:T(256)S(1)}, s32[193]{0:T(256)}, u32[]{:S(2)}) copy-start(s32[193]{0:T(256)} %get-tuple-element.8.slots_ref) | copy-start | bytes 2320
  92.7 42.1 %all-to-all-start.2 = ((bf16[16,32,1024]{2,1,0:T(8,128)(2,1)}), bf16[16,32,1024]{2,1,0:T(8,128)(2,1)S(1)}, u32[]{:S(2)}, u32[]{:S(2)}) async-start(bf16[16,32,1024]{2,1,0:T(8,128)(2,1)} %bitcast.6), calls=%async_computation.2 | async-start | bytes 2097152 | tf_op jit(solution)/shard_map/all_to_all | solution.py:343
  96.4 1.6 copy-start.4
  134.8 44.4 %all-to-all-start.1 = ((bf16[16,32,1024]{2,1,0:T(8,128)(2,1)}), bf16[16,32,1024]{2,1,0:T(8,128)(2,1)S(1)}, u32[]{:S(2)}, u32[]{:S(2)}) async-start(bf16[16,32,1024]{2,1,0:T(8,128)(2,1)} %bitcast.4), calls=%async_computation.1 | async-start | bytes 2097152 | tf_op jit(solution)/shard_map/all_to_all | solution.py:343
  140.7 1.6 copy-start.5
  142.3 42.8 %copy-start.2 = (s32[193]{0:T(256)S(1)}, s32[193]{0:T(256)}, u32[]{:S(2)}) copy-start(s32[193]{0:T(256)} %get-tuple-element.7.returns_ref) | copy-start | bytes 2320
  178.1 1.0 copy-start
  179.1 29.0 %all-to-all-start = ((bf16[16,32,1024]{2,1,0:T(8,128)(2,1)}), bf16[16,32,1024]{2,1,0:T(8,128)(2,1)S(1)}, u32[]{:S(2)}, u32[]{:S(2)}) async-start(bf16[16,32,1024]{2,1,0:T(8,128)(2,1)} %bitcast.21), calls=%async_computation | async-start | bytes 2097152 | tf_op jit(solution)/shard_map/all_to_all | solution.py:343
Sparse Core Ops, SparseCore 0:
  9.5 44.1 all-gather.3

commit v5 on v4

--- a/solution.py
+++ b/solution.py
@@ -108,10 +108,10 @@
 
 
 def profile_kernel(
-    part, depth, touches, slots_ref, local_ref, query_ref, library_ref, out_ref,
-    cand_ref, spectrum_ref, left_ref, right_ref,
+    part, depth, touches, slots_ref, local_ref, query_ref, library_ref, out_ref, *scratch
 ):
     per_touch = 8
+    sets = [scratch[i::2] for i in range(2)]
     rows = 2 * per_touch
     blocks = query_ref.shape[1]
     offsets = SHIFTS // LANES
@@ -123,8 +123,9 @@
     lane = lax.broadcasted_iota(jnp.int32, (8, LANES), 1)
     lane16 = lax.broadcasted_iota(jnp.int32, (rows, LANES), 1)
 
-    cand_ref[...] = jnp.zeros(cand_ref.shape, cand_ref.dtype)
-    right_ref[...] = jnp.zeros(right_ref.shape, right_ref.dtype)
+    for cand_ref, _, _, right_ref in sets:
+        cand_ref[...] = jnp.zeros(cand_ref.shape, cand_ref.dtype)
+        right_ref[...] = jnp.zeros(right_ref.shape, right_ref.dtype)
 
     def choose(pieces):
         value = pieces[0]
@@ -132,7 +133,7 @@
             value = jnp.where(lane16 < group * WIDTH, value, pieces[group])
         return value
 
-    def gather(slot, half):
+    def gather(cand_ref, slot, half):
         place = slot // part_depth * depth + part * part_depth + slot % part_depth
         touch = jnp.maximum(slots_ref[place], 0)
         for k in range(per_touch):
@@ -147,7 +148,7 @@
         mean = jnp.sum(square, axis=1, keepdims=True) / (blocks * LANES)
         return touch // touches, lax.rsqrt(mean + EPSILON)
 
-    def make_left():
+    def make_left(cand_ref, left_ref):
         pieces = [
             cand_ref[pl.ds(rows * b, rows), :].astype(jnp.bfloat16)
             for b in range(blocks + offsets + 1)
@@ -163,7 +164,7 @@
                     [turned[(g - a) % GROUPS] for g in range(GROUPS)]
                 )
 
-    def make_right(query, half):
+    def make_right(spectrum_ref, right_ref, query, half):
         spectrum_ref[half] = query_ref[query].astype(jnp.float32)
         zero = jnp.zeros((8, LANES), jnp.float32)
         before = (zero, zero)
@@ -189,7 +190,7 @@
                 )
             before, before_shifted = now, shifted
 
-    def sums(low, high):
+    def sums(left_ref, right_ref, low, high):
         left = jnp.concatenate(
             [
                 jnp.concatenate(
@@ -205,14 +206,20 @@
         )
         return jnp.dot(left, right_ref[...], preferred_element_type=jnp.float32)
 
-    @pl.loop(0, part_slots // 2)
-    def _(pair):
-        queries, scales = zip(*[gather(2 * pair + half, half) for half in range(2)])
-        make_left()
+    def make(pair, refs):
+        cand_ref, spectrum_ref, left_ref, right_ref = refs
+        found = [gather(cand_ref, 2 * pair + half, half) for half in range(2)]
+        make_left(cand_ref, left_ref)
         for half in range(2):
-            make_right(queries[half], half)
+            make_right(spectrum_ref, right_ref, found[half][0], half)
+        return tuple(scale for _, scale in found)
+
+    def finish(pair, scales, refs):
+        left_ref, right_ref = refs[2:]
         step = GROUPS // CHAINS
-        products = [sums(step * c, step * (c + 1)) for c in range(CHAINS)]
+        products = [
+            sums(left_ref, right_ref, step * c, step * (c + 1)) for c in range(CHAINS)
+        ]
 
         def found(a, o, half):
             at = ((a % step) * (offsets + 1) + o) * rows + half * per_touch
@@ -236,6 +243,17 @@
                 jnp.concatenate(both, axis=0).astype(jnp.bfloat16)
             )
 
+    pairs = part_slots // 2
+
+    def two(i, scales):
+        following = make(2 * i + 1, sets[1])
+        finish(2 * i, scales, sets[0])
+        scales = make(jnp.minimum(2 * i + 2, pairs - 1), sets[0])
+        finish(2 * i + 1, following, sets[1])
+        return scales
+
+    lax.fori_loop(0, pairs // 2, two, make(0, sets[0]))
+
 
 def profile(part, depth, touches, devices, slots, local, queries, library):
     blocks = queries.shape[1]
@@ -251,10 +269,14 @@
         in_specs=[smem, smem, vmem, vmem],
         out_specs=vmem,
         scratch_shapes=[
-            pltpu.VMEM(((blocks + offsets + 1) * 16, LANES), jnp.float32),
-            pltpu.VMEM((2, blocks, LANES), jnp.float32),
-            pltpu.VMEM((GROUPS, (tiles + offsets + 1) * 16, LANES), jnp.bfloat16),
-            pltpu.VMEM(((tiles + 1) * LANES, 2 * LANES), jnp.bfloat16),
+            buffer
+            for buffer in (
+                pltpu.VMEM(((blocks + offsets + 1) * 16, LANES), jnp.float32),
+                pltpu.VMEM((2, blocks, LANES), jnp.float32),
+                pltpu.VMEM((GROUPS, (tiles + offsets + 1) * 16, LANES), jnp.bfloat16),
+                pltpu.VMEM(((tiles + 1) * LANES, 2 * LANES), jnp.bfloat16),
+            )
+            for _ in range(2)
         ],
         compiler_params=pltpu.CompilerParams(vmem_limit_bytes=VMEM_LIMIT),
         cost_estimate=pl.CostEstimate(

time: 221 us -> 280 us (1.27)
  Pallas kernels: 134 us -> 194 us
    pallas_call x3, Pallas kernels: 109 us -> 169 us  [profile(): pl.pallas_call(functools.partial(profile_kernel, part, depth, touches), o...]
  transfers between devices with their start and end apart: 4 -> 4, of which waited for: 2 -> 2; matrix products, arithmetic and copies ran while one was open for 4% -> 3% of each run, Pallas kernels for 42% -> 47%
where the time goes in v5:
time: 280 us; the launch traced here: 279 us
  Pallas kernels  194 us (69%)
  blocking collectives  23.3 us (8%)
  waiting for transfers between devices  17.1 us (6%)
  starting transfers between devices  15.6 us (6%)
  local copies, waits for them, and re-layouts  15.2 us (5%)
  between operations  13.6 us (5%)
    pallas_call x3, Pallas kernels, profile(): pl.pallas_call(functools.partial(profile_kernel, part, depth, touches), o...  169 us
    all_gather x1, blocking collectives, local(): lax.all_gather(jnp.concatenate([own, cand_local.reshape(-1)]), 'lib', axi...  23.3 us
    all_to_all x3, starting transfers between devices, local(): got = lax.all_to_all(answer, 'lib', split_axis=0, concat_axis=0, tiled=True)  15.6 us
    all_to_all x3, waiting for transfers between devices, local(): got = lax.all_to_all(answer, 'lib', split_axis=0, concat_axis=0, tiled=True)  15.4 us
    unnamed x25, local copies, waits for them, and re-layouts  14.4 us
    pallas_call x1, Pallas kernels, route(): pl.pallas_call(functools.partial(route_kernel, num_query, touches, depth)...  11.6 us
    pallas_call x3, Pallas kernels, unpack(): pl.pallas_call(functools.partial(unpack_kernel, part, depth), out_shape=j...  11.2 us
  transfers between devices with their start and end apart: 4, of which 2 were waited for; matrix products, arithmetic and copies ran while one was open for 3% of the time, Pallas kernels for 47%

profile of v5, /device:TPU:0, one launch (start us, length us, event | category | flops | bytes accessed | tf_op | source)
XLA Modules:
  0.0 278.6 jit_solution(9881794397659566708)
XLA Ops:
  6.5 0.0 all-gather.4.cloned.1.call-start
  6.5 0.9 copy-done.1
  7.4 1.8 prepare.1
  9.2 0.0 all-gather.4.cloned.1.call-update
  9.3 0.8 copy.10
  10.0 0.1 reshape.42.own_ref
  10.1 0.8 copy.11
  11.0 0.1 reshape.43
  11.1 23.3 %all-gather.1 = s32[16,1,1152]{2,1,0:T(1,128)S(1)} all-gather(s32[1,1,1152]{2,1,0:T(1,128)S(1)} %reshape.55), channel_id=2, replica_groups=mesh['groups'=2,'lib'=16] {'lib'}, dimensions={0}, use_global_device_ids=true | all-gather | bytes 78336 | tf_op jit(solution)/shard_map/all_gather | solution.py:351
  34.4 5.5 %copy.14 = bf16[64,8,32,128]{3,2,1,0:T(8,128)(2,1)} copy(bf16[64,8,32,128]{3,1,2,0:T(8,128)(2,1)} %bitcast.25) | data formatting | bytes 8388608
  39.9 0.6 slice_bitcast_fusion.1.named_ref
  40.5 11.6 %route.1 = (s32[193]{0:T(256)}, s32[193]{0:T(256)}) custom-call(s32[1]{0:T(128)} %bitcast.me_ref, s32[2048]{0:T(1024)} %slice_bitcast_fusion.1.named_ref, s32[128]{0:T(128)} %copy-done.8), custom_call_target="tpu_custom_call" | custom-call | tf_op jit(solution)/shard_map/route/pallas_call | solution.py:101
  52.1 1.6 all-gather.4.cloned.1.call-done.query_ref
  53.7 1.6 copy-done.3
  55.3 0.6 copy-done.6
  55.9 56.7 %profile_0.1 = bf16[512,1024]{1,0:T(8,128)(2,1)} custom-call(s32[193]{0:T(256)S(1)} %copy-done.6, s32[16384]{0:T(1024)S(1)} %bitcast.22, bf16[256,32,128]{2,1,0:T(8,128)(2,1)S(1)} %copy-done.3, bf16[512,32,128]{2,1,0:T(8,128)(2,1)} %bitcast.26), custom_call_target="tpu_custom_call" | custom-call | flops 43486543872 | bytes 8388608 | tf_op jit(solution)/shard_map/profile_0/pallas_call | solution.py:266
  112.6 3.7 %all-to-all-start.2 = ((bf16[16,32,1024]{2,1,0:T(8,128)(2,1)}), bf16[16,32,1024]{2,1,0:T(8,128)(2,1)S(1)}, u32[]{:S(2)}, u32[]{:S(2)}) async-start(bf16[16,32,1024]{2,1,0:T(8,128)(2,1)} %bitcast.6), calls=%async_computation.2 | async-start | bytes 2097152 | tf_op jit(solution)/shard_map/all_to_all | solution.py:365
  116.3 0.0 copy-done.7
  116.3 0.0 copy-start.4
  116.3 1.6 copy-done.4
  117.9 56.8 %profile_1.1 = bf16[512,1024]{1,0:T(8,128)(2,1)} custom-call(s32[193]{0:T(256)S(1)} %copy-done.7, s32[16384]{0:T(1024)S(1)} %bitcast.23, bf16[256,32,128]{2,1,0:T(8,128)(2,1)S(1)} %copy-done.4, bf16[512,32,128]{2,1,0:T(8,128)(2,1)} %bitcast.27), custom_call_target="tpu_custom_call" | custom-call | flops 43486543872 | bytes 8388608 | tf_op jit(solution)/shard_map/profile_1/pallas_call | solution.py:266
  174.7 0.0 all-to-all-done.2
  174.7 6.0 %all-to-all-start.1 = ((bf16[16,32,1024]{2,1,0:T(8,128)(2,1)}), bf16[16,32,1024]{2,1,0:T(8,128)(2,1)S(1)}, u32[]{:S(2)}, u32[]{:S(2)}) async-start(bf16[16,32,1024]{2,1,0:T(8,128)(2,1)} %bitcast.4), calls=%async_computation.1 | async-start | bytes 2097152 | tf_op jit(solution)/shard_map/all_to_all | solution.py:365
  180.7 1.6 copy-done.5
  182.2 55.8 %profile_2.1 = bf16[512,1024]{1,0:T(8,128)(2,1)S(1)} custom-call(s32[193]{0:T(256)S(1)} %copy-done.7, s32[16384]{0:T(1024)S(1)} %bitcast.24, bf16[256,32,128]{2,1,0:T(8,128)(2,1)S(1)} %copy-done.5, bf16[512,32,128]{2,1,0:T(8,128)(2,1)} %bitcast.28), custom_call_target="tpu_custom_call" | custom-call | flops 43486543872 | bytes 8388608 | tf_op jit(solution)/shard_map/profile_2/pallas_call | solution.py:266
  238.0 1.0 copy-done
  239.0 0.0 all-to-all-done.1
  239.0 6.0 %all-to-all-start = ((bf16[16,32,1024]{2,1,0:T(8,128)(2,1)}), bf16[16,32,1024]{2,1,0:T(8,128)(2,1)S(1)}, u32[]{:S(2)}, u32[]{:S(2)}) async-start(bf16[16,32,1024]{2,1,0:T(8,128)(2,1)} %bitcast.21), calls=%async_computation | async-start | bytes 2097152 | tf_op jit(solution)/shard_map/all_to_all | solution.py:365
  245.0 3.7 %unpack_0.1.rest_0_ = f32[128,8,1024]{2,1,0:T(8,128)} custom-call(s32[193]{0:T(256)S(1)} %copy-done.2, bf16[64,8,1024]{2,1,0:T(8,128)(2,1)S(1)} %bitcast.20), custom_call_target="tpu_custom_call" | custom-call | bytes 3145728 | tf_op jit(solution)/shard_map/unpack_0/pallas_call | solution.py:324
  248.8 3.8 %unpack_1.1.rest_0_ = f32[128,8,1024]{2,1,0:T(8,128)} custom-call(s32[193]{0:T(256)S(1)} %copy-done.2, bf16[64,8,1024]{2,1,0:T(8,128)(2,1)S(1)} %bitcast.18, f32[128,8,1024]{2,1,0:T(8,128)} %unpack_0.1.rest_0_), custom_call_target="tpu_custom_call", output_to_operand_aliasing={{}: (2, {})} | custom-call | bytes 3145728 | tf_op jit(solution)/shard_map/unpack_1/pallas_call | solution.py:324
  252.5 15.4 %all-to-all-done = bf16[16,32,1024]{2,1,0:T(8,128)(2,1)S(1)} async-done(((bf16[16,32,1024]{2,1,0:T(8,128)(2,1)}), bf16[16,32,1024]{2,1,0:T(8,128)(2,1)S(1)}, u32[]{:S(2)}, u32[]{:S(2)}) %all-to-all-start) | async-done | bytes 1048608 | tf_op jit(solution)/shard_map/all_to_all | solution.py:365
  268.0 3.7 %unpack_2.1 = f32[128,8,1024]{2,1,0:T(8,128)} custom-call(s32[193]{0:T(256)S(1)} %copy-done.2, bf16[64,8,1024]{2,1,0:T(8,128)(2,1)S(1)} %bitcast.19, f32[128,8,1024]{2,1,0:T(8,128)} %unpack_1.1.rest_0_), custom_call_target="tpu_custom_call", output_to_operand_aliasing={{}: (2, {})} | custom-call | bytes 3145728 | tf_op jit(solution)/shard_map/unpack_2/pallas_call | solution.py:324
  (15 shorter events, 0.1 us)
Async XLA Ops:
  6.5 47.1 %all-gather.4.cloned.1.call-start = ((), (), s32[]{:S(2)}) async-start(), calls=%async_computation.3 | async-start | bytes 2228224 | tf_op jit(solution)/shard_map/all_gather | solution.py:355
  6.5 0.9 copy-start.1
  10.1 29.8 %copy-start.8 = (s32[128]{0:T(128)}, s32[128]{0:T(128)S(1)}, u32[]{:S(2)}) copy-start(s32[128]{0:T(128)S(1)} %reshape.42.own_ref) | copy-start | bytes 1540
  53.7 1.6 copy-start.3
  55.3 0.6 copy-start.6
  55.9 60.4 %copy-start.7 = (s32[193]{0:T(256)S(1)}, s32[193]{0:T(256)}, u32[]{:S(2)}) copy-start(s32[193]{0:T(256)} %get-tuple-element.8.slots_ref) | copy-start | bytes 2320
  112.6 62.0 %all-to-all-start.2 = ((bf16[16,32,1024]{2,1,0:T(8,128)(2,1)}), bf16[16,32,1024]{2,1,0:T(8,128)(2,1)S(1)}, u32[]{:S(2)}, u32[]{:S(2)}) async-start(bf16[16,32,1024]{2,1,0:T(8,128)(2,1)} %bitcast.6), calls=%async_computation.2 | async-start | bytes 2097152 | tf_op jit(solution)/shard_map/all_to_all | solution.py:365
  116.3 1.6 copy-start.4
  174.7 64.3 %all-to-all-start.1 = ((bf16[16,32,1024]{2,1,0:T(8,128)(2,1)}), bf16[16,32,1024]{2,1,0:T(8,128)(2,1)S(1)}, u32[]{:S(2)}, u32[]{:S(2)}) async-start(bf16[16,32,1024]{2,1,0:T(8,128)(2,1)} %bitcast.4), calls=%async_computation.1 | async-start | bytes 2097152 | tf_op jit(solution)/shard_map/all_to_all | solution.py:365
  180.6 1.6 copy-start.5
  182.2 62.8 %copy-start.2 = (s32[193]{0:T(256)S(1)}, s32[193]{0:T(256)}, u32[]{:S(2)}) copy-start(s32[193]{0:T(256)} %get-tuple-element.7.returns_ref) | copy-start | bytes 2320
  238.0 1.0 copy-start
  239.0 29.0 %all-to-all-start = ((bf16[16,32,1024]{2,1,0:T(8,128)(2,1)}), bf16[16,32,1024]{2,1,0:T(8,128)(2,1)S(1)}, u32[]{:S(2)}, u32[]{:S(2)}) async-start(bf16[16,32,1024]{2,1,0:T(8,128)(2,1)} %bitcast.21), calls=%async_computation | async-start | bytes 2097152 | tf_op jit(solution)/shard_map/all_to_all | solution.py:365
Sparse Core Ops, SparseCore 0:
  9.5 44.1 all-gather.3
